TPU v7x, 32 devices: a whole 2x2x4 slice. The times are simulated.
32 devices in a mesh: box: 8 (over z, core), dir: 4 (over y, x).
Axes of the slice: x: 2, y: 2, z: 4, core: 2. Of those that a mesh axis runs over, the one named last changes fastest.
Arguments:
- child_spectra: bfloat16 [256, 24, 48, 256], P(('box', 'dir')), may hold values from -6 to 6
- child_ids: int32 [256], P('box'), may hold values from 0 to 511, as said below
- translators: bfloat16 [2, 316, 48, 96], P(None, None, None, 'dir'), may hold values from -0.75 to 0.75
- trans_index: int32 [64, 64], replicated, may hold values from 0 to 316
Outputs:
- parent_spectra: bfloat16 [64, 48, 96, 256], P('box', None, 'dir')
- incoming: bfloat16 [64, 48, 96, 256], P('box', None, 'dir')
Inputs may be any that keep to these rules, and one draw needn't show every extreme that they name: child_ids never fall; every parent index below 64 has 1 to 8 children with distinct octants, and each box row has a parent with all 8; the children on box row r (positions r * 32 to (r+1) * 32 - 1) belong to parents r * 8 to (r+1) * 8 - 1, except 1 to 3 last ones on every row but the last, which belong to parent (r+1) * 8. `trans_index`: 0 marks a pair without translation; k > 0 selects operator k - 1.
All inputs are finite; a program needn't handle non-finite values.
Results may differ from a plain program's by a relative error of at most 0.0069.
Values may be sent and summed in bfloat16 or wider, within the bound.
A program may use at most 128 MiB of HBM per device.

v0:
```python
import jax
import jax.numpy as jnp
import numpy as np
from jax import lax
from jax.sharding import PartitionSpec as P

wave_shift = 5.0
midpoint_taps = (3.0, -25.0, 150.0, 150.0, -25.0, 3.0)


def with_halo(block, sides, width):
    for axis, dim in sides:
        count = lax.axis_size(axis)
        forward = [(i, i + 1) for i in range(count - 1)]
        forward.append((count - 1, 0))
        backward = [(target, source) for source, target in forward]
        low = lax.ppermute(
            lax.slice_in_dim(block, block.shape[dim] - width, None, axis=dim), axis, forward
        )
        high = lax.ppermute(lax.slice_in_dim(block, 0, width, axis=dim), axis, backward)
        block = jnp.concatenate([low, block, high], axis=dim)
    return block


def passed_along(value, axis, steps):
    count = lax.axis_size(axis)
    first, last = (max(0, -steps), min(count, count - steps))
    return lax.ppermute(value, axis, [(source, source + steps) for source in range(first, last)])


def theta_table(coarse_count):
    fine_count = 2 * coarse_count
    table_rows = np.zeros((fine_count, coarse_count))
    for target in range(fine_count):
        position = target / 2.0 - 0.25
        window_start = min(max(int(np.floor(position)) - 2, 0), coarse_count - 6)
        for tap_index in range(6):
            weight_value = 1.0
            for other_tap in range(6):
                if other_tap != tap_index:
                    weight_value *= (position - window_start - other_tap) / (tap_index - other_tap)
            table_rows[target, window_start + tap_index] = weight_value
    return table_rows


def local_phi_table(local_count):
    table_rows = np.zeros((2 * local_count, local_count + 6))
    for target in range(2 * local_count):
        if target % 2 == 0:
            table_rows[target, target // 2 + 3] = 1.0
        else:
            middle = (target - 1) // 2
            for offset in range(6):
                table_rows[target, middle + 1 + offset] = midpoint_taps[offset] / 256.0
    return table_rows


def phase_factors(octants, theta_count, phi_angles):
    theta_angles = jnp.pi * (jnp.arange(theta_count, dtype=jnp.float32) + 0.5) / theta_count
    sign_x = ((octants % 2).astype(jnp.float32) * 2.0 - 1.0)[:, None, None]
    sign_y = ((octants // 2 % 2).astype(jnp.float32) * 2.0 - 1.0)[:, None, None]
    sign_z = ((octants // 4).astype(jnp.float32) * 2.0 - 1.0)[:, None, None]
    sine_theta = jnp.sin(theta_angles)[None, :, None]
    cosine_theta = jnp.cos(theta_angles)[None, :, None]
    angle_sum = wave_shift * (
        sign_x * sine_theta * jnp.cos(phi_angles)[None, None, :]
        + sign_y * sine_theta * jnp.sin(phi_angles)[None, None, :]
        + sign_z * cosine_theta
    )
    return (jnp.cos(angle_sum), jnp.sin(angle_sum))


def rotate(lifted, cosine, sine):
    half = lifted.shape[-1] // 2
    real_part = lifted[..., :half]
    imag_part = lifted[..., half:]
    cosine = cosine[..., None]
    sine = sine[..., None]
    return jnp.concatenate(
        [cosine * real_part - sine * imag_part, sine * real_part + cosine * imag_part], axis=-1
    )


def apply_operators(operators, sources):
    direct = jnp.einsum(
        "pqtf,qtfr->ptfr", operators[0], sources, preferred_element_type=jnp.float32
    )
    cross = jnp.einsum("pqtf,qtfr->ptfr", operators[1], sources, preferred_element_type=jnp.float32)
    half = direct.shape[-1] // 2
    return jnp.concatenate(
        [direct[..., :half] - cross[..., half:], direct[..., half:] + cross[..., :half]], axis=-1
    )


def local(child_spectra, child_ids, translators, trans_index):
    columns = lax.all_to_all(child_spectra, "dir", split_axis=2, concat_axis=0, tiled=True)
    padded = with_halo(columns, (("dir", 2),), 3)
    row_children = columns.shape[0]
    theta_coarse = columns.shape[1]
    local_coarse = columns.shape[2]
    width_last = columns.shape[3]
    theta_fine = 2 * theta_coarse
    local_fine = 2 * local_coarse
    parent_rows = row_children // 4
    box_rank = lax.axis_index("box")
    dir_rank = lax.axis_index("dir")
    phi_weights = jnp.asarray(local_phi_table(local_coarse), jnp.float32).astype(jnp.bfloat16)
    theta_weights = jnp.asarray(theta_table(theta_coarse), jnp.float32).astype(jnp.bfloat16)
    phi_index = (dir_rank * local_fine + jnp.arange(local_fine, dtype=jnp.int32)).astype(
        jnp.float32
    )
    phi_angles = 2.0 * jnp.pi * phi_index / (local_fine * lax.axis_size("dir"))
    slot_local = child_ids // 8 - box_rank * parent_rows
    octants = child_ids % 8
    group_size = 8
    group_count = row_children // group_size
    block_inputs = (
        padded.reshape(group_count, group_size, theta_coarse, local_coarse + 6, width_last),
        octants.reshape(group_count, group_size),
        slot_local.reshape(group_count, group_size),
    )
    slot_range = jnp.arange(parent_rows + 1, dtype=jnp.int32)

    def advance(accumulated, block_data):
        spectra_block, octant_block, slot_block = block_data
        widened = jnp.einsum(
            "ctjr,gj->ctgr", spectra_block, phi_weights, preferred_element_type=jnp.float32
        ).astype(jnp.bfloat16)
        lifted = jnp.einsum(
            "ctgr,ht->chgr", widened, theta_weights, preferred_element_type=jnp.float32
        )
        cosine, sine = phase_factors(octant_block, theta_fine, phi_angles)
        shifted = rotate(lifted, cosine, sine).astype(jnp.bfloat16)
        onehot = (slot_range[:, None] == slot_block[None, :]).astype(jnp.bfloat16)
        accumulated = accumulated + jnp.einsum(
            "sc,chgr->shgr", onehot, shifted, preferred_element_type=jnp.float32
        )
        return (accumulated, None)

    start_sums = jnp.zeros((parent_rows + 1, theta_fine, local_fine, width_last), jnp.float32)
    slot_sums, unused = lax.scan(advance, start_sums, block_inputs)
    ghost_sum = passed_along(slot_sums[parent_rows:], "box", 1)
    own_sums = slot_sums[:parent_rows] + jnp.pad(
        ghost_sum, ((0, parent_rows - 1), (0, 0), (0, 0), (0, 0))
    )
    parent_spectra = own_sums.astype(jnp.bfloat16)
    padded_table = jnp.concatenate(
        [jnp.zeros((2, 1, theta_fine, local_fine), jnp.bfloat16), translators], axis=1
    )
    relaid = lax.all_to_all(parent_spectra, "box", split_axis=1, concat_axis=0, tiled=True)
    theta_local = relaid.shape[1]
    table_slice = lax.dynamic_slice_in_dim(padded_table, box_rank * theta_local, theta_local, 2)
    operators = jnp.take(table_slice, trans_index, axis=1)
    product = apply_operators(operators, relaid).astype(jnp.bfloat16)
    incoming = lax.all_to_all(product, "box", split_axis=0, concat_axis=1, tiled=True)
    return (parent_spectra, incoming)


def solution(mesh):
    return jax.shard_map(
        local,
        mesh=mesh,
        in_specs=(P(("box", "dir"), None, None, None), P("box"), P(None, None, None, "dir"), P()),
        out_specs=(P("box", None, "dir", None), P("box", None, "dir", None)),
        check_vma=False,
    )
```

profile of v0, /device:TPU:16, one launch (start us, length us, event | category | flops | bytes accessed | tf_op | source)
XLA Modules:
  0.0 505.4 jit_solution(15921697238447897756)
XLA Ops:
  0.6 4.0 copy.37
  4.6 57.0 %all_to_all.54 = bf16[8,24,48,256]{3,1,0,2:T(8,128)(2,1)S(1)} all-to-all(bf16[8,24,48,256]{3,1,0,2:T(8,128)(2,1)S(1)} %copy.37), channel_id=1, replica_groups=mesh['box'=8,'dir'=4] {'dir'}, dimensions={2} | all-to-all | bytes 9437184 | tf_op jit(solution)/shard_map/all_to_all | solution.py:96
  70.7 24.3 %collective-permute-done = bf16[32,24,3,256]{3,1,2,0:T(8,128)(2,1)S(1)} collective-permute-done((bf16[32,24,3,256]{3,1,2,0:T(8,128)(2,1)}, bf16[32,24,3,256]{3,1,2,0:T(8,128)(2,1)S(1)}, u32[]{:S(2)}, u32[]{:S(2)}) %collective-permute-start) | collective-permute-done | bytes 1179680 | tf_op jit(solution)/shard_map/ppermute | solution.py:17
  95.0 22.3 %collective-permute-done.1 = bf16[32,24,3,256]{3,1,2,0:T(8,128)(2,1)S(1)} collective-permute-done((bf16[32,24,3,256]{3,1,2,0:T(8,128)(2,1)S(1)}, bf16[32,24,3,256]{3,1,2,0:T(8,128)(2,1)S(1)}, u32[]{:S(2)}, u32[]{:S(2)}) %collective-permute-start.1) | collective-permute-done | bytes 1179680 | tf_op jit(solution)/shard_map/ppermute | solution.py:20
  120.7 100.2 %while.16 = (s32[]{:T(128)}, f32[9,48,24,256]{3,0,2,1:T(8,128)}, s32[4,8]{1,0:T(4,128)S(1)}, s32[4,8]{1,0:T(4,128)S(1)}, bf16[4,8,24,18,256]{4,2,3,0,1:T(8,128)(...) while((s32[]{:T(128)}, f32[9,48,24,256]{3,0,2,1:T(8,128)}, ...), condition=%wide.region_1.2_spmd.clone.clone.clone, body=%wide.region_0.1_spmd.clone.clone.clone.sunk | while | flops 223591264 | bytes 69170944 | solution.py:141
  131.0 12.7 %select_add_fusion.2 = f32[9,48,24,256]{3,0,2,1:T(8,128)} fusion(f32[9,48,24,256]{3,0,2,1:T(8,128)} %get-tuple-element.372, pred[]{:T(512)S(6)} %compare.36, bf16[8,48,24,256]{3,1,2,0:T(8,128)(2,1)} %pad_maximum_fusion.4, s32[8]{0:T(128)S(1)} %fusion.71), kind=kOutput, calls=%fused_computation.6.clone.1 | convolution fusion | flops 47775816 | bytes 25952288 | tf_op jit(solution)/shard_map/while/body/eval_jaxpr/sc,chgr->shgr/dot_general | solution.py:135
  154.0 15.4 %select_add_fusion.2 = f32[9,48,24,256]{3,0,2,1:T(8,128)} fusion(f32[9,48,24,256]{3,0,2,1:T(8,128)} %get-tuple-element.372, pred[]{:T(512)S(6)} %compare.36, bf16[8,48,24,256]{3,1,2,0:T(8,128)(2,1)} %pad_maximum_fusion.4, s32[8]{0:T(128)S(1)} %fusion.71), kind=kOutput, calls=%fused_computation.6.clone.1 | convolution fusion | flops 47775816 | bytes 25952288 | tf_op jit(solution)/shard_map/while/body/eval_jaxpr/sc,chgr->shgr/dot_general | solution.py:135
  179.8 15.4 %select_add_fusion.2 = f32[9,48,24,256]{3,0,2,1:T(8,128)} fusion(f32[9,48,24,256]{3,0,2,1:T(8,128)} %get-tuple-element.372, pred[]{:T(512)S(6)} %compare.36, bf16[8,48,24,256]{3,1,2,0:T(8,128)(2,1)} %pad_maximum_fusion.4, s32[8]{0:T(128)S(1)} %fusion.71), kind=kOutput, calls=%fused_computation.6.clone.1 | convolution fusion | flops 47775816 | bytes 25952288 | tf_op jit(solution)/shard_map/while/body/eval_jaxpr/sc,chgr->shgr/dot_general | solution.py:135
  205.5 15.4 %select_add_fusion.2 = f32[9,48,24,256]{3,0,2,1:T(8,128)} fusion(f32[9,48,24,256]{3,0,2,1:T(8,128)} %get-tuple-element.372, pred[]{:T(512)S(6)} %compare.36, bf16[8,48,24,256]{3,1,2,0:T(8,128)(2,1)} %pad_maximum_fusion.4, s32[8]{0:T(128)S(1)} %fusion.71), kind=kOutput, calls=%fused_computation.6.clone.1 | convolution fusion | flops 47775816 | bytes 25952288 | tf_op jit(solution)/shard_map/while/body/eval_jaxpr/sc,chgr->shgr/dot_general | solution.py:135
  220.9 20.3 %copy.43 = f32[9,48,24,256]{3,2,0,1:T(8,128)} copy(f32[9,48,24,256]{3,0,2,1:T(8,128)} %get-tuple-element.172) | data formatting | bytes 21233664 | tf_op jit(solution)/shard_map/while | solution.py:141
  244.5 15.6 %collective-permute-done.2 = f32[1,48,24,256]{3,2,0,1:T(8,128)S(1)} collective-permute-done((f32[1,48,24,256]{3,2,0,1:T(8,128)S(1)}, f32[1,48,24,256]{3,2,0,1:T(8,128)S(1)}, u32[]{:S(2)}, u32[]{:S(2)}) %collective-permute-start.2) | collective-permute-done | bytes 1179680 | tf_op jit(solution)/shard_map/ppermute | solution.py:28
  260.1 6.6 %fusion.29 = bf16[8,48,24,256]{3,2,0,1:T(8,128)(2,1)} fusion(f32[9,48,24,256]{3,2,0,1:T(8,128)} %copy.43, f32[1,48,24,256]{3,2,0,1:T(8,128)S(1)} %collective-permute-done.2), kind=kLoop, calls=%fused_computation.57 | loop fusion | flops 4718592 | bytes 15335424 | tf_op jit(solution)/shard_map/convert_element_type | solution.py:146
  266.7 5.4 %all-to-all-start.1 = ((bf16[8,48,24,256]{3,2,0,1:T(8,128)(2,1)}), bf16[8,48,24,256]{3,2,0,1:T(8,128)(2,1)}, u32[]{:S(2)}, u32[]{:S(2)}) async-start(bf16[8,48,24,256]{3,2,0,1:T(8,128)(2,1)} %fusion.29), calls=%async_computation.1 | async-start | bytes 9437184 | tf_op jit(solution)/shard_map/all_to_all | solution.py:150
  272.1 12.2 %copy.46 = bf16[2,316,48,24]{3,0,2,1:T(2,128)(2,1)} copy(bf16[2,316,48,24]{1,3,2,0:T(8,128)(2,1)S(1)} %copy-done.2) | data formatting | bytes 2912256 | tf_op args[2]
  286.7 51.6 %gather_fusion = bf16[4096,2,6,24]{3,1,2,0:T(2,128)(2,1)} fusion(bf16[2,317,6,24]{3,0,2,1:T(2,128)(2,1)S(1)} %pad_dynamic-slice_fusion, s32[4096]{0:T(1024)S(1)} %broadcast_clamp_fusion), kind=kCustom, calls=%fused_computation | custom fusion | bytes 4734976 | tf_op jit(solution)/shard_map/jit(_take)/gather | solution.py:153
  338.3 30.9 %copy.55 = bf16[64,64,2,6,24]{1,0,4,3,2:T(8,128)(2,1)} copy(bf16[64,64,2,6,24]{4,2,3,1,0:T(2,128)(2,1)} %bitcast.91) | data formatting | bytes 4718592 | tf_op jit(solution)/shard_map/jit(_take)/gather | solution.py:153
  369.2 5.0 select_bitcast_fusion
  374.1 4.6 fusion.38
  378.7 3.7 fusion.41
  385.7 4.9 copy.48
  390.6 7.8 %all-to-all-start.2 = ((bf16[64,6,24,256]{3,2,1,0:T(8,128)(2,1)}), bf16[64,6,24,256]{3,2,1,0:T(8,128)(2,1)}, u32[]{:S(2)}, u32[]{:S(2)}) async-start(bf16[64,6,24,256]{3,2,1,0:T(8,128)(2,1)} %copy.48), calls=%async_computation.2 | async-start | bytes 9437184 | tf_op jit(solution)/shard_map/all_to_all | solution.py:155
  398.4 4.8 copy.50
  403.3 97.1 %all-to-all-done.2 = bf16[64,6,24,256]{3,2,1,0:T(8,128)(2,1)} async-done(((bf16[64,6,24,256]{3,2,1,0:T(8,128)(2,1)}), bf16[64,6,24,256]{3,2,1,0:T(8,128)(2,1)}, u32[]{:S(2)}, u32[]{:S(2)}) %all-to-all-start.2) | async-done | bytes 4718624 | tf_op jit(solution)/shard_map/all_to_all | solution.py:155
  500.4 5.0 copy.49
  (86 shorter events, 62.5 us)
Async XLA Ops:
  61.6 2.2 copy-start
  63.8 4.1 copy-start.6
  65.0 30.0 %collective-permute-start = (bf16[32,24,3,256]{3,1,2,0:T(8,128)(2,1)}, bf16[32,24,3,256]{3,1,2,0:T(8,128)(2,1)S(1)}, u32[]{:S(2)}, u32[]{:S(2)}) collective-permute-start(bf16[32,24,3,256]{3,1,2,0:T(8,128)(2,1)} %get-tuple-element.294), channel_id=1, source_target_pairs={{0,1},{1,2},{2,3},{3,0},{4,5},{5,6},{6,7},{7,4},{8,9},{9,10},{10,1... | collective-permute-start | bytes 3538952 | tf_op jit(solution)/shard_map/ppermute | solution.py:17
  65.9 51.4 %collective-permute-start.1 = (bf16[32,24,3,256]{3,1,2,0:T(8,128)(2,1)S(1)}, bf16[32,24,3,256]{3,1,2,0:T(8,128)(2,1)S(1)}, u32[]{:S(2)}, u32[]{:S(2)}) collective-permute-start(bf16[32,24,3,256]{3,1,2,0:T(8,128)(2,1)S(1)} %get-tuple-element.295), channel_id=1, source_target_pairs={{1,0},{2,1},{3,2},{0,3},{5,4},{6,5},{7,6},{4,7},{9,8},{10,9},{11,1... | collective-permute-start | bytes 3538952 | tf_op jit(solution)/shard_map/ppermute | solution.py:20
  117.3 3.3 copy-start.3
  117.3 3.3 copy-start.4
  242.6 17.5 %collective-permute-start.2 = (f32[1,48,24,256]{3,2,0,1:T(8,128)S(1)}, f32[1,48,24,256]{3,2,0,1:T(8,128)S(1)}, u32[]{:S(2)}, u32[]{:S(2)}) collective-permute-start(f32[1,48,24,256]{3,2,0,1:T(8,128)S(1)} %slice.67), channel_id=1, source_target_pairs={{0,4},{4,8},{8,12},{12,16},{16,20},{20,24},{24,28},{1,5},{5,9},{9,... | collective-permute-start | bytes 3538952 | tf_op jit(solution)/shard_map/ppermute | solution.py:28
  266.7 5.4 %copy-start.2 = (bf16[2,316,48,24]{1,3,2,0:T(8,128)(2,1)S(1)}, bf16[2,316,48,24]{1,3,2,0:T(8,128)(2,1)}, u32[]{:S(2)}) copy-start(bf16[2,316,48,24]{1,3,2,0:T(8,128)(2,1)} %param.10) | copy-start | bytes 4368388
  266.7 107.4 %all-to-all-start.1 = ((bf16[8,48,24,256]{3,2,0,1:T(8,128)(2,1)}), bf16[8,48,24,256]{3,2,0,1:T(8,128)(2,1)}, u32[]{:S(2)}, u32[]{:S(2)}) async-start(bf16[8,48,24,256]{3,2,0,1:T(8,128)(2,1)} %fusion.29), calls=%async_computation.1 | async-start | bytes 9437184 | tf_op jit(solution)/shard_map/all_to_all | solution.py:150
  272.1 12.2 %copy-start.5 = (s32[64,64]{1,0:T(8,128)S(1)}, s32[64,64]{1,0:T(8,128)}, u32[]{:S(2)}) copy-start(s32[64,64]{1,0:T(8,128)} %param.11) | copy-start | bytes 49156
  374.1 4.6 copy-start.1
  390.6 109.8 %all-to-all-start.2 = ((bf16[64,6,24,256]{3,2,1,0:T(8,128)(2,1)}), bf16[64,6,24,256]{3,2,1,0:T(8,128)(2,1)}, u32[]{:S(2)}, u32[]{:S(2)}) async-start(bf16[64,6,24,256]{3,2,1,0:T(8,128)(2,1)} %copy.48), calls=%async_computation.2 | async-start | bytes 9437184 | tf_op jit(solution)/shard_map/all_to_all | solution.py:155
where the time goes:
time: 511 us; the launch traced here: 505 us
  waiting for transfers between devices  159 us (31%)
  local copies, waits for them, and re-layouts  150 us (29%)
  matrix products  75.9 us (15%)
  blocking collectives  57 us (11%)
  other arithmetic  44.2 us (9%)
  starting transfers between devices  18 us (4%)
    all_to_all x1, waiting for transfers between devices, local(): lax.all_to_all(product, 'box', split_axis=0, concat_axis=1, tiled=True)  97.1 us
    gather x2, local copies, waits for them, and re-layouts, local(): operators = jnp.take(table_slice, trans_index, axis=1)  82.5 us
    dot_general x4, matrix products, advance(): jnp.einsum('sc,chgr->shgr', onehot, shifted, preferred_element_type=jnp.f...  58.9 us
    all_to_all x1, blocking collectives, local(): lax.all_to_all(child_spectra, 'dir', split_axis=2, concat_axis=0, tiled=T...  57 us
    ppermute x1, waiting for transfers between devices, with_halo(): lax.ppermute(lax.slice_in_dim(block, block.shape[dim] - width, None, axis...  24.3 us
    unnamed x17, local copies, waits for them, and re-layouts  22.7 us
    ppermute x1, waiting for transfers between devices, with_halo(): lax.ppermute(lax.slice_in_dim(block, 0, width, axis=dim), axis, backward)  22.3 us
    while x1, local copies, waits for them, and re-layouts, local(): slot_sums, unused = lax.scan(advance, start_sums, block_inputs)  20.3 us
  transfers between devices with their start and end apart: 5, of which 4 were waited for; matrix products, arithmetic and copies ran while one was open for 22% of the time, Pallas kernels for 0%

commit v1 on v0

v1 whole, which is shorter than its diff:
```python
import functools

import jax
import jax.numpy as jnp
import ml_dtypes
import numpy as np
from jax import lax
from jax.experimental import pallas as pl
from jax.experimental.pallas import tpu as pltpu
from jax.sharding import PartitionSpec as P

wave_shift = 5.0
midpoint_taps = (3.0, -25.0, 150.0, 150.0, -25.0, 3.0)
halo = 3
straddle = 3


def theta_table(coarse_count):
    fine_count = 2 * coarse_count
    table_rows = np.zeros((fine_count, coarse_count))
    for target in range(fine_count):
        position = target / 2.0 - 0.25
        window_start = min(max(int(np.floor(position)) - 2, 0), coarse_count - 6)
        for tap_index in range(6):
            weight_value = 1.0
            for other_tap in range(6):
                if other_tap != tap_index:
                    weight_value *= (position - window_start - other_tap) / (tap_index - other_tap)
            table_rows[target, window_start + tap_index] = weight_value
    return table_rows


def local_phi_table(local_count):
    table_rows = np.zeros((2 * local_count, local_count + 2 * halo))
    for target in range(2 * local_count):
        if target % 2 == 0:
            table_rows[target, target // 2 + halo] = 1.0
        else:
            middle = (target - 1) // 2
            for offset in range(6):
                table_rows[target, middle + 1 + offset] = midpoint_taps[offset] / 256.0
    return table_rows


def phase_factors(octants, theta_count, phi_angles):
    theta_angles = jnp.pi * (jnp.arange(theta_count, dtype=jnp.float32) + 0.5) / theta_count
    sign_x = ((octants % 2).astype(jnp.float32) * 2.0 - 1.0)[:, None, None]
    sign_y = ((octants // 2 % 2).astype(jnp.float32) * 2.0 - 1.0)[:, None, None]
    sign_z = ((octants // 4).astype(jnp.float32) * 2.0 - 1.0)[:, None, None]
    sine_theta = jnp.sin(theta_angles)[None, :, None]
    cosine_theta = jnp.cos(theta_angles)[None, :, None]
    angle_sum = wave_shift * (
        sign_x * sine_theta * jnp.cos(phi_angles)[None, None, :]
        + sign_y * sine_theta * jnp.sin(phi_angles)[None, None, :]
        + sign_z * cosine_theta
    )
    return (jnp.cos(angle_sum), jnp.sin(angle_sum))


def lift_kernel(pieces, group, parents, targets, slots, octants, *refs):
    blocks = refs[:pieces]
    ghosts = refs[pieces : 2 * pieces]
    weights = refs[2 * pieces : 3 * pieces]
    cosine, sine, out, send, total = refs[3 * pieces :]
    half = out.shape[-1] // 2
    step = pl.program_id(0)

    def add_child(position, sources, index):
        slot = slots[position]

        @pl.when((slot >= 0) & (slot < parents))
        def _():
            lifted = None
            for source, weight in zip(sources, weights):
                part = jnp.dot(weight[...], source[index], preferred_element_type=jnp.float32)
                lifted = part if lifted is None else lifted + part
            octant = octants[position]
            turn_cos = cosine[octant]
            turn_sin = sine[octant]
            real_part = lifted[:, :half]
            imag_part = lifted[:, half:]
            total[slot, :, :half] += turn_cos * real_part - turn_sin * imag_part
            total[slot, :, half:] += turn_sin * real_part + turn_cos * imag_part

    @pl.when(step == 0)
    def _():
        total[...] = jnp.zeros_like(total)

        @pl.loop(0, straddle)
        def _(index):
            add_child(index, ghosts, index)

    @pl.loop(0, group)
    def _(index):
        add_child(straddle + step * group + index, blocks, index)

    @pl.when(step == pl.num_programs(0) - 1)
    def _():
        rows = send.shape[2]
        for parent in range(parents):
            values = total[parent].astype(out.dtype)
            out[parent] = values
            for target in range(targets):
                send[target, parent] = values[target * rows : (target + 1) * rows]


def lift(pieces, ghosts, weights, cosine, sine, slots, octants, parents, targets):
    children = pieces[0].shape[0]
    group = 8
    rows = weights[0].shape[0]
    width = pieces[0].shape[-1]
    count = len(pieces)

    def whole(array):
        zeros = (0,) * array.ndim
        return pl.BlockSpec(array.shape, lambda step, *_: zeros)

    in_specs = [
        pl.BlockSpec((group,) + piece.shape[1:], lambda step, *_: (step, 0, 0)) for piece in pieces
    ]
    in_specs += [whole(array) for array in (*ghosts, *weights, cosine, sine)]
    out_shape = [
        jax.ShapeDtypeStruct((parents, rows, width), jnp.bfloat16),
        jax.ShapeDtypeStruct((targets, parents, rows // targets, width), jnp.bfloat16),
    ]
    flops = 2 * children * rows * width * sum(w.shape[1] for w in weights)
    return pl.pallas_call(
        functools.partial(lift_kernel, count, group, parents, targets),
        grid_spec=pltpu.PrefetchScalarGridSpec(
            num_scalar_prefetch=2,
            grid=(children // group,),
            in_specs=in_specs,
            out_specs=[whole(shape) for shape in out_shape],
            scratch_shapes=[pltpu.VMEM((parents, rows, width), jnp.float32)],
        ),
        out_shape=out_shape,
        compiler_params=pltpu.CompilerParams(vmem_limit_bytes=48 * 2**20),
        cost_estimate=pl.CostEstimate(
            flops=4 * flops, bytes_accessed=sum(p.size for p in pieces) * 2, transcendentals=0
        ),
        name="lift",
    )(slots, octants, *pieces, *ghosts, *weights, cosine, sine)


def translate_kernel(operators, sources, out):
    half = out.shape[-1] // 2
    for index in range(out.shape[0]):
        spectra = sources[index]
        direct = jnp.dot(operators[0, index], spectra, preferred_element_type=jnp.float32)
        cross = jnp.dot(operators[1, index], spectra, preferred_element_type=jnp.float32)
        out[index, :, :half] = (direct[:, :half] - cross[:, half:]).astype(out.dtype)
        out[index, :, half:] = (direct[:, half:] + cross[:, :half]).astype(out.dtype)


def translate(operators, sources):
    points, parents, width = sources.shape
    group = next(size for size in (8, 6, 4, 3, 2, 1) if points % size == 0)
    return pl.pallas_call(
        translate_kernel,
        grid=(points // group,),
        in_specs=[
            pl.BlockSpec((2, group, parents, parents), lambda step: (0, step, 0, 0)),
            pl.BlockSpec((group, parents, width), lambda step: (step, 0, 0)),
        ],
        out_specs=pl.BlockSpec((group, parents, width), lambda step: (step, 0, 0)),
        out_shape=jax.ShapeDtypeStruct(sources.shape, jnp.bfloat16),
        cost_estimate=pl.CostEstimate(
            flops=16 * points * parents * parents * width,
            bytes_accessed=8 * sources.size,
            transcendentals=0,
        ),
        name="translate",
    )(operators, sources)


def shared_out(block, ways):
    local_count = block.shape[2] // ways
    ring = jnp.concatenate([block[:, :, -halo:], block, block[:, :, :halo]], axis=2)
    width = local_count + 2 * halo
    parts = [ring[:, :, way * local_count : way * local_count + width] for way in range(ways)]
    stacked = jnp.stack(parts)
    return stacked.reshape(ways, block.shape[0], block.shape[1] * width, block.shape[3])


def chunk_plan(coarse_count, chunks):
    table = theta_table(coarse_count)
    fine_chunk = 2 * coarse_count // chunks
    needed = []
    for chunk in range(chunks):
        used = np.nonzero(table[chunk * fine_chunk : (chunk + 1) * fine_chunk].any(axis=0))[0]
        needed.append((int(used[0]), int(used[-1]) + 1))
    starts = [0] + [end for _, end in needed[:-1]]
    return [(start, end) for start, (_, end) in zip(starts, needed)], needed


def local(child_spectra, child_ids, translators, trans_index):
    ways = lax.axis_size("dir")
    rows = lax.axis_size("box")
    theta_coarse, phi_coarse, width = child_spectra.shape[1:]
    row_children = child_ids.shape[0]
    theta_fine = 2 * theta_coarse
    local_coarse = phi_coarse // ways
    local_fine = 2 * local_coarse
    parents_all = trans_index.shape[0]
    parents = parents_all // rows
    chunks = next(count for count in (3, 2, 1) if theta_fine % (count * rows) == 0)
    fine_chunk = theta_fine // chunks
    theta_local = fine_chunk // rows
    points = theta_local * local_fine
    box_rank = lax.axis_index("box")
    dir_rank = lax.axis_index("dir")
    segments, needed = chunk_plan(theta_coarse, chunks)

    forward = [(source, source + 1) for source in range(rows - 1)]
    ghost_ids = lax.ppermute(child_ids[-straddle:], "box", forward)
    ghost_ids = jnp.where(box_rank > 0, ghost_ids, -8)
    all_ids = jnp.concatenate([ghost_ids, child_ids])
    slots = all_ids // 8 - box_rank * parents
    octants = all_ids % 8

    columns, ghosts = [], []
    for start, end in segments:
        sent = shared_out(child_spectra[:, start:end], ways)
        got = lax.all_to_all(sent, "dir", split_axis=0, concat_axis=0, tiled=True)
        got = got.reshape((row_children,) + got.shape[2:])
        columns.append(got)
        ghosts.append(lax.ppermute(got[-straddle:], "box", forward))

    phi_index = (dir_rank * local_fine + jnp.arange(local_fine, dtype=jnp.int32)).astype(
        jnp.float32
    )
    phi_angles = 2.0 * jnp.pi * phi_index / (local_fine * ways)
    cosine, sine = phase_factors(jnp.arange(8, dtype=jnp.int32), theta_fine, phi_angles)

    def lanes(table, chunk):
        part = table[:, chunk * fine_chunk : (chunk + 1) * fine_chunk]
        part = part.reshape(8, fine_chunk * local_fine, 1)
        return jnp.broadcast_to(part, part.shape[:2] + (width // 2,))

    theta_weights = theta_table(theta_coarse).astype(ml_dtypes.bfloat16).astype(np.float64)
    phi_weights = local_phi_table(local_coarse)

    count = translators.shape[1]
    split = translators.reshape(2, count, chunks, rows, theta_local, local_fine)
    own = lax.dynamic_index_in_dim(split, box_rank, 3, keepdims=False)
    own = own.transpose(0, 2, 3, 4, 1).reshape(2 * chunks * points, count)
    chosen = trans_index.reshape(1, -1) - 1 == jnp.arange(count, dtype=jnp.int32)[:, None]
    operators = jnp.dot(own, chosen.astype(jnp.bfloat16), preferred_element_type=jnp.float32)
    operators = operators.astype(jnp.bfloat16)
    operators = operators.reshape(2, chunks, points, parents_all, parents_all)

    own_parts, sent_parts = [], []
    for chunk in range(chunks):
        low, high = needed[chunk]
        used = [
            index for index, (start, end) in enumerate(segments) if start < high and end > low
        ]
        weights = []
        for index in used:
            start, end = segments[index]
            table = np.einsum(
                "ht,gj->hgtj",
                theta_weights[chunk * fine_chunk : (chunk + 1) * fine_chunk, start:end],
                phi_weights,
            )
            table = table.reshape(fine_chunk * local_fine, -1)
            weights.append(jnp.asarray(table.astype(ml_dtypes.bfloat16)))
        part, sent = lift(
            [columns[index] for index in used],
            [ghosts[index] for index in used],
            weights,
            lanes(cosine, chunk),
            lanes(sine, chunk),
            slots,
            octants,
            parents,
            rows,
        )
        own_parts.append(part.reshape(parents, fine_chunk, local_fine, width))
        sent_parts.append(sent)

    results = []
    for chunk in range(chunks):
        got = lax.all_to_all(sent_parts[chunk], "box", split_axis=0, concat_axis=0, tiled=True)
        got = got.reshape(parents_all, points, width).transpose(1, 0, 2)
        moved = translate(operators[:, chunk], got).transpose(1, 0, 2)
        moved = moved.reshape(rows, parents, points, width)
        back = lax.all_to_all(moved, "box", split_axis=0, concat_axis=0, tiled=True)
        back = back.transpose(1, 0, 2, 3)
        results.append(back.reshape(parents, fine_chunk, local_fine, width))
    return jnp.concatenate(own_parts, axis=1), jnp.concatenate(results, axis=1)


def solution(mesh):
    return jax.shard_map(
        local,
        mesh=mesh,
        in_specs=(P(("box", "dir"), None, None, None), P("box"), P(None, None, None, "dir"), P()),
        out_specs=(P("box", None, "dir", None), P("box", None, "dir", None)),
        check_vma=False,
    )
```

time: 511 us -> 380 us (0.74)
  matrix products: 75.9 us -> 2.93 us
  local copies, waits for them, and re-layouts: 150 us -> 83.8 us
  blocking collectives: 57 us -> 0 us
  Pallas kernels: 0 us -> 49.8 us
  starting transfers between devices: 18 us -> 63.1 us
  other arithmetic: 44.2 us -> 14.1 us
    gather x2 -> x0, local copies, waits for them, and re-layouts: 82.5 us -> none  [local(): operators = jnp.take(table_slice, trans_index, axis=1)]
    dot_general x14 -> x1, matrix products: 75.9 us -> 2.93 us  [local(): jnp.dot(own, chosen.astype(jnp.bfloat16), preferred_element_type=jnp.floa...]
    all_to_all x1 -> x0, blocking collectives: 57 us -> none  [local(): lax.all_to_all(child_spectra, 'dir', split_axis=2, concat_axis=0, tiled=T...]
    pallas_call x0 -> x6, Pallas kernels: none -> 49.8 us  [the longest x3 33.3 us: lift(): pl.pallas_call(functools.partial(lift_kernel, count, group, parents, targ...]
    all_to_all x2 -> x9, starting transfers between devices: 13.1 us -> 53.5 us  [the longest x3 22.7 us: local(): back = lax.all_to_all(moved, 'box', split_axis=0, concat_axis=0, tiled=True)]
    all_to_all x2 -> x9, waiting for transfers between devices: 97.1 us -> 126 us  [the longest x3 72.7 us: local(): back = lax.all_to_all(moved, 'box', split_axis=0, concat_axis=0, tiled=True)]
    ppermute x3 -> x4, waiting for transfers between devices: 62.2 us -> 33.3 us  [the longest x3 33.3 us: local(): ghosts.append(lax.ppermute(got[-straddle:], 'box', forward))]
    reshape x2 -> x7, local copies, waits for them, and re-layouts: 0.17 us -> 22.1 us  [the longest x3 8.04 us: local(): moved = moved.reshape(rows, parents, points, width)]
  transfers between devices with their start and end apart: 5 -> 13, of which waited for: 4 -> 10; matrix products, arithmetic and copies ran while one was open for 22% -> 22% of each run, Pallas kernels for 0% -> 13%
where the time goes in v1:
time: 380 us; the launch traced here: 374 us
  waiting for transfers between devices  159 us (42%)
  local copies, waits for them, and re-layouts  83.8 us (22%)
  starting transfers between devices  63.1 us (17%)
  Pallas kernels  49.8 us (13%)
  other arithmetic  14.1 us (4%)
    all_to_all x3, waiting for transfers between devices, local(): back = lax.all_to_all(moved, 'box', split_axis=0, concat_axis=0, tiled=True)  72.7 us
    ppermute x3, waiting for transfers between devices, local(): ghosts.append(lax.ppermute(got[-straddle:], 'box', forward))  33.3 us
    pallas_call x3, Pallas kernels, lift(): pl.pallas_call(functools.partial(lift_kernel, count, group, parents, targ...  33.3 us
    all_to_all x3, waiting for transfers between devices, local(): lax.all_to_all(sent_parts[chunk], 'box', split_axis=0, concat_axis=0, til...  27.6 us
    all_to_all x3, waiting for transfers between devices, local(): got = lax.all_to_all(sent, 'dir', split_axis=0, concat_axis=0, tiled=True)  25.8 us
    all_to_all x3, starting transfers between devices, local(): back = lax.all_to_all(moved, 'box', split_axis=0, concat_axis=0, tiled=True)  22.7 us
    all_to_all x3, starting transfers between devices, local(): lax.all_to_all(sent_parts[chunk], 'box', split_axis=0, concat_axis=0, til...  17.2 us
    pallas_call x3, Pallas kernels, translate(): pl.pallas_call(translate_kernel, grid=(points // group,), in_specs=[pl.Bl...  16.6 us
  transfers between devices with their start and end apart: 13, of which 10 were waited for; matrix products, arithmetic and copies ran while one was open for 22% of the time, Pallas kernels for 13%

profile of v1, /device:TPU:16, one launch (start us, length us, event | category | flops | bytes accessed | tf_op | source)
XLA Modules:
  0.0 374.2 jit_solution(11880335245383637800)
XLA Ops:
  17.3 11.2 %all-to-all-done.2 = bf16[4,8,90,256]{3,1,2,0:T(8,128)(2,1)} async-done(((bf16[4,8,90,256]{3,1,2,0:T(8,128)(2,1)}), bf16[4,8,90,256]{3,1,2,0:T(8,128)(2,1)}, u32[]{:S(2)}, u32[]{:S(2)}) %all-to-all-start.2) | async-done | bytes 1474592 | tf_op jit(solution)/shard_map/all_to_all | solution.py:224
  28.5 4.5 %all-to-all-start.1 = ((bf16[4,8,144,256]{3,1,2,0:T(8,128)(2,1)}), bf16[4,8,144,256]{3,1,2,0:T(8,128)(2,1)}, u32[]{:S(2)}, u32[]{:S(2)}) async-start(bf16[4,8,144,256]{3,1,2,0:T(8,128)(2,1)} %pad_maximum_fusion.3), calls=%async_computation.1 | async-start | bytes 4718592 | tf_op jit(solution)/shard_map/all_to_all | solution.py:224
  51.3 9.0 %all-to-all-done.1 = bf16[4,8,144,256]{3,1,2,0:T(8,128)(2,1)} async-done(((bf16[4,8,144,256]{3,1,2,0:T(8,128)(2,1)}), bf16[4,8,144,256]{3,1,2,0:T(8,128)(2,1)}, u32[]{:S(2)}, u32[]{:S(2)}) %all-to-all-start.1) | async-done | bytes 2359328 | tf_op jit(solution)/shard_map/all_to_all | solution.py:224
  60.3 4.7 %all-to-all-start = ((bf16[4,8,198,256]{3,1,2,0:T(8,128)(2,1)}), bf16[4,8,198,256]{3,1,2,0:T(8,128)(2,1)}, u32[]{:S(2)}, u32[]{:S(2)}) async-start(bf16[4,8,198,256]{3,1,2,0:T(8,128)(2,1)} %pad_maximum_fusion.2), calls=%async_computation | async-start | bytes 6488064 | tf_op jit(solution)/shard_map/all_to_all | solution.py:224
  83.4 11.5 %lift.5 = (bf16[8,384,256]{2,1,0:T(8,128)(2,1)S(1)}, bf16[8,8,48,256]{3,2,1,0:T(8,128)(2,1)S(1)}) custom-call(s32[35]{0:T(128)S(1)} %fusion.13.slots, s32[35]{0:T(128)S(1)} %get-tuple-element.14.octants, bf16[32,144,256]{2,1,0:T(8,128)(2,1)} %bitcast.90, bf16[32,90,256]{2,1,0:T(8,128)(2,1)S(1)} %bitcast.72, ...), custom_call_target="tpu_custom_call" | custom-call | flops 5888802816 | bytes 3833856 | tf_op jit(solution)/shard_map/lift/pallas_call | solution.py:127
  96.0 5.6 %all-to-all-done = bf16[4,8,198,256]{3,1,2,0:T(8,128)(2,1)} async-done(((bf16[4,8,198,256]{3,1,2,0:T(8,128)(2,1)}), bf16[4,8,198,256]{3,1,2,0:T(8,128)(2,1)}, u32[]{:S(2)}, u32[]{:S(2)}) %all-to-all-start) | async-done | bytes 3244064 | tf_op jit(solution)/shard_map/all_to_all | solution.py:224
  101.7 5.2 %all-to-all-start.7 = ((bf16[8,8,48,256]{3,2,1,0:T(8,128)(2,1)}), bf16[8,8,48,256]{3,2,1,0:T(8,128)(2,1)}, u32[]{:S(2)}, u32[]{:S(2)}) async-start(bf16[8,8,48,256]{3,2,1,0:T(8,128)(2,1)} %copy-done.4), calls=%async_computation.7 | async-start | bytes 3145728 | tf_op jit(solution)/shard_map/all_to_all | solution.py:284
  115.6 29.9 %collective-permute-done.1.refs_1_.refs_2_ = bf16[3,198,256]{2,1,0:T(8,128)(2,1)} collective-permute-done((bf16[3,198,256]{2,1,0:T(8,128)(2,1)}, bf16[3,198,256]{2,1,0:T(8,128)(2,1)}, u32[]{:S(2)}, u32[]{:S(2)}) %collective-permute-start.1) | collective-permute-done | bytes 304160 | tf_op jit(solution)/shard_map/ppermute | solution.py:227
  148.4 11.6 %lift.4 = (bf16[8,384,256]{2,1,0:T(8,128)(2,1)S(1)}, bf16[8,8,48,256]{3,2,1,0:T(8,128)(2,1)S(1)}) custom-call(s32[35]{0:T(128)S(1)} %fusion.13.slots, s32[35]{0:T(128)S(1)} %get-tuple-element.14.octants, bf16[32,198,256]{2,1,0:T(8,128)(2,1)} %bitcast.83, bf16[32,144,256]{2,1,0:T(8,128)(2,1)} %bitcast.91, ...), custom_call_target="tpu_custom_call" | custom-call | flops 8606711808 | bytes 5603328 | tf_op jit(solution)/shard_map/lift/pallas_call | solution.py:127
  169.0 10.1 %lift.3 = (bf16[8,384,256]{2,1,0:T(8,128)(2,1)S(1)}, bf16[8,8,48,256]{3,2,1,0:T(8,128)(2,1)S(1)}) custom-call(s32[35]{0:T(128)S(1)} %fusion.13.slots, s32[35]{0:T(128)S(1)} %get-tuple-element.14.octants, bf16[32,198,256]{2,1,0:T(8,128)(2,1)} %bitcast.84, bf16[3,198,256]{2,1,0:T(8,128)(2,1)} %collective-permute-done.1.refs_1_.refs_2_, ...), custom_call_target="tpu_custom_call" | custom-call | flops 4982833152 | bytes 3244032 | tf_op jit(solution)/shard_map/lift/pallas_call | solution.py:127
  181.4 19.8 %all-to-all-done.5 = bf16[8,8,48,256]{3,2,1,0:T(8,128)(2,1)} async-done(((bf16[8,8,48,256]{3,2,1,0:T(8,128)(2,1)}), bf16[8,8,48,256]{3,2,1,0:T(8,128)(2,1)}, u32[]{:S(2)}, u32[]{:S(2)}) %all-to-all-start.5) | async-done | bytes 1572896 | tf_op jit(solution)/shard_map/all_to_all | solution.py:284
  201.2 7.7 %all-to-all-start.3 = ((bf16[8,8,48,256]{3,2,1,0:T(8,128)(2,1)}), bf16[8,8,48,256]{3,2,1,0:T(8,128)(2,1)}, u32[]{:S(2)}, u32[]{:S(2)}) async-start(bf16[8,8,48,256]{3,2,1,0:T(8,128)(2,1)} %copy-done.3), calls=%async_computation.3 | async-start | bytes 3145728 | tf_op jit(solution)/shard_map/all_to_all | solution.py:284
  211.9 7.6 %reshape.281 = bf16[2,3,48,64,64]{4,3,2,1,0:T(8,128)(2,1)} reshape(bf16[288,4096]{1,0:T(8,128)(2,1)} %convolution_convert_fusion) | data formatting | bytes 4718592 | tf_op jit(solution)/shard_map/reshape | solution.py:250
  219.5 4.9 %slice_bitcast_fusion.2 = (bf16[2,48,64,64]{3,2,1,0:T(8,128)(2,1)}, bf16[2,48,64,64]{3,2,1,0:T(8,128)(2,1)}, bf16[2,48,64,64]{3,2,1,0:T(8,128)(2,1)}) fusion(bf16[2,3,48,64,64]{4,3,2,1,0:T(8,128)(2,1)} %reshape.281), kind=kLoop, calls=%fused_computation.9 | loop fusion | bytes 4718592 | tf_op jit(solution)/shard_map/squeeze | solution.py:286
  227.5 5.5 %translate.5 = bf16[48,64,256]{2,1,0:T(8,128)(2,1)} custom-call(bf16[2,48,64,64]{3,2,1,0:T(8,128)(2,1)} %get-tuple-element.18.operators, bf16[48,64,256]{2,1,0:T(8,128)(2,1)} %bitcast.77), custom_call_target="tpu_custom_call" | custom-call | flops 805306368 | bytes 6291456 | tf_op jit(solution)/shard_map/translate/pallas_call | solution.py:158
  235.7 7.8 %all-to-all-done.3 = bf16[8,8,48,256]{3,2,1,0:T(8,128)(2,1)} async-done(((bf16[8,8,48,256]{3,2,1,0:T(8,128)(2,1)}), bf16[8,8,48,256]{3,2,1,0:T(8,128)(2,1)}, u32[]{:S(2)}, u32[]{:S(2)}) %all-to-all-start.3) | async-done | bytes 1572896 | tf_op jit(solution)/shard_map/all_to_all | solution.py:284
  243.5 7.6 %all-to-all-start.8 = ((bf16[8,8,48,256]{3,1,2,0:T(8,128)(2,1)}), bf16[8,8,48,256]{3,1,2,0:T(8,128)(2,1)}, u32[]{:S(2)}, u32[]{:S(2)}) async-start(bf16[8,8,48,256]{3,1,2,0:T(8,128)(2,1)} %copy.70), calls=%async_computation.8 | async-start | bytes 3145728 | tf_op jit(solution)/shard_map/all_to_all | solution.py:288
  254.1 5.5 %translate.4 = bf16[48,64,256]{2,1,0:T(8,128)(2,1)} custom-call(bf16[2,48,64,64]{3,2,1,0:T(8,128)(2,1)} %get-tuple-element.17.operators, bf16[48,64,256]{2,1,0:T(8,128)(2,1)} %bitcast.79), custom_call_target="tpu_custom_call" | custom-call | flops 805306368 | bytes 6291456 | tf_op jit(solution)/shard_map/translate/pallas_call | solution.py:158
  262.3 23.3 %all-to-all-done.8 = bf16[8,8,48,256]{3,1,2,0:T(8,128)(2,1)} async-done(((bf16[8,8,48,256]{3,1,2,0:T(8,128)(2,1)}), bf16[8,8,48,256]{3,1,2,0:T(8,128)(2,1)}, u32[]{:S(2)}, u32[]{:S(2)}) %all-to-all-start.8) | async-done | bytes 1572896 | tf_op jit(solution)/shard_map/all_to_all | solution.py:288
  285.6 7.6 %all-to-all-start.6 = ((bf16[8,8,48,256]{3,1,2,0:T(8,128)(2,1)}), bf16[8,8,48,256]{3,1,2,0:T(8,128)(2,1)}, u32[]{:S(2)}, u32[]{:S(2)}) async-start(bf16[8,8,48,256]{3,1,2,0:T(8,128)(2,1)} %copy.67), calls=%async_computation.6 | async-start | bytes 3145728 | tf_op jit(solution)/shard_map/all_to_all | solution.py:288
  296.2 5.5 %translate.3 = bf16[48,64,256]{2,1,0:T(8,128)(2,1)} custom-call(bf16[2,48,64,64]{3,2,1,0:T(8,128)(2,1)} %get-tuple-element.16.operators, bf16[48,64,256]{2,1,0:T(8,128)(2,1)} %bitcast.76), custom_call_target="tpu_custom_call" | custom-call | flops 805306368 | bytes 6291456 | tf_op jit(solution)/shard_map/translate/pallas_call | solution.py:158
  304.5 23.2 %all-to-all-done.6 = bf16[8,8,48,256]{3,1,2,0:T(8,128)(2,1)} async-done(((bf16[8,8,48,256]{3,1,2,0:T(8,128)(2,1)}), bf16[8,8,48,256]{3,1,2,0:T(8,128)(2,1)}, u32[]{:S(2)}, u32[]{:S(2)}) %all-to-all-start.6) | async-done | bytes 1572896 | tf_op jit(solution)/shard_map/all_to_all | solution.py:288
  327.7 7.6 %all-to-all-start.4 = ((bf16[8,8,48,256]{3,1,2,0:T(8,128)(2,1)}), bf16[8,8,48,256]{3,1,2,0:T(8,128)(2,1)}, u32[]{:S(2)}, u32[]{:S(2)}) async-start(bf16[8,8,48,256]{3,1,2,0:T(8,128)(2,1)} %copy.64), calls=%async_computation.4 | async-start | bytes 3145728 | tf_op jit(solution)/shard_map/all_to_all | solution.py:288
  343.7 26.1 %all-to-all-done.4 = bf16[8,8,48,256]{3,1,2,0:T(8,128)(2,1)} async-done(((bf16[8,8,48,256]{3,1,2,0:T(8,128)(2,1)}), bf16[8,8,48,256]{3,1,2,0:T(8,128)(2,1)}, u32[]{:S(2)}, u32[]{:S(2)}) %all-to-all-start.4) | async-done | bytes 1572896 | tf_op jit(solution)/shard_map/all_to_all | solution.py:288
  (127 shorter events, 109.9 us)
Async XLA Ops:
  0.6 208.4 %copy-start = (bf16[2,316,48,24]{1,3,2,0:T(8,128)(2,1)S(1)}, bf16[2,316,48,24]{1,3,2,0:T(8,128)(2,1)}, u32[]{:S(2)}) copy-start(bf16[2,316,48,24]{1,3,2,0:T(8,128)(2,1)} %param.11) | copy-start | bytes 4368388
  5.7 22.9 %all-to-all-start.2 = ((bf16[4,8,90,256]{3,1,2,0:T(8,128)(2,1)}), bf16[4,8,90,256]{3,1,2,0:T(8,128)(2,1)}, u32[]{:S(2)}, u32[]{:S(2)}) async-start(bf16[4,8,90,256]{3,1,2,0:T(8,128)(2,1)} %pad_maximum_fusion.4), calls=%async_computation.2 | async-start | bytes 2949120 | tf_op jit(solution)/shard_map/all_to_all | solution.py:224
  10.0 3.7 copy-start.13
  17.3 15.7 %copy-start.18 = (s32[32]{0:T(128)S(1)}, s32[32]{0:T(128)}, u32[]{:S(2)}) copy-start(s32[32]{0:T(128)} %param.10) | copy-start | bytes 388
  28.5 31.8 %all-to-all-start.1 = ((bf16[4,8,144,256]{3,1,2,0:T(8,128)(2,1)}), bf16[4,8,144,256]{3,1,2,0:T(8,128)(2,1)}, u32[]{:S(2)}, u32[]{:S(2)}) async-start(bf16[4,8,144,256]{3,1,2,0:T(8,128)(2,1)} %pad_maximum_fusion.3), calls=%async_computation.1 | async-start | bytes 4718592 | tf_op jit(solution)/shard_map/all_to_all | solution.py:224
  33.7 33.2 %collective-permute-start = (s32[3]{0:T(128)}, s32[3]{0:T(128)S(1)}, u32[]{:S(2)}, u32[]{:S(2)}) collective-permute-start(s32[3]{0:T(128)} %slice.120), channel_id=1, source_target_pairs={{0,4},{4,8},{8,12},{12,16},{16,20},{20,24},{24,28},{1,5},{5,9},{9,... | collective-permute-start | bytes 44 | tf_op jit(solution)/shard_map/ppermute | solution.py:215
  60.3 41.4 %all-to-all-start = ((bf16[4,8,198,256]{3,1,2,0:T(8,128)(2,1)}), bf16[4,8,198,256]{3,1,2,0:T(8,128)(2,1)}, u32[]{:S(2)}, u32[]{:S(2)}) async-start(bf16[4,8,198,256]{3,1,2,0:T(8,128)(2,1)} %pad_maximum_fusion.2), calls=%async_computation | async-start | bytes 6488064 | tf_op jit(solution)/shard_map/all_to_all | solution.py:224
  68.7 8.0 %collective-permute-start.3 = (bf16[3,90,256]{2,1,0:T(8,128)(2,1)S(1)}, bf16[3,90,256]{2,1,0:T(8,128)(2,1)S(1)}, u32[]{:S(2)}, u32[]{:S(2)}) collective-permute-start(bf16[3,90,256]{2,1,0:T(8,128)(2,1)S(1)} %slice.160), channel_id=1, source_target_pairs={{0,4},{4,8},{8,12},{12,16},{16,20},{20,24},{24,28},{1,5},{5,9},{9,... | collective-permute-start | bytes 414728 | tf_op jit(solution)/shard_map/ppermute | solution.py:227
  72.8 10.6 %copy-start.16 = (bf16[4,8,144,256]{3,2,1,0:T(8,128)(2,1)}, bf16[4,8,144,256]{3,2,1,0:T(8,128)(2,1)S(1)}, u32[]{:S(2)}) copy-start(bf16[4,8,144,256]{3,2,1,0:T(8,128)(2,1)S(1)} %copy.55) | copy-start | bytes 7077892
  72.8 7.3 %collective-permute-start.2 = (bf16[3,144,256]{2,1,0:T(8,128)(2,1)S(1)}, bf16[3,144,256]{2,1,0:T(8,128)(2,1)S(1)}, u32[]{:S(2)}, u32[]{:S(2)}) collective-permute-start(bf16[3,144,256]{2,1,0:T(8,128)(2,1)S(1)} %slice.157), channel_id=1, source_target_pairs={{0,4},{4,8},{8,12},{12,16},{16,20},{20,24},{24,28},{1,5},{5,9},{9,... | collective-permute-start | bytes 663560 | tf_op jit(solution)/shard_map/ppermute | solution.py:227
  80.1 3.3 copy-start.6
  80.1 3.3 copy-start.11
  80.1 3.3 copy-start.12
  101.7 60.8 %all-to-all-start.7 = ((bf16[8,8,48,256]{3,2,1,0:T(8,128)(2,1)}), bf16[8,8,48,256]{3,2,1,0:T(8,128)(2,1)}, u32[]{:S(2)}, u32[]{:S(2)}) async-start(bf16[8,8,48,256]{3,2,1,0:T(8,128)(2,1)} %copy-done.4), calls=%async_computation.7 | async-start | bytes 3145728 | tf_op jit(solution)/shard_map/all_to_all | solution.py:284
  111.9 33.6 %collective-permute-start.1 = (bf16[3,198,256]{2,1,0:T(8,128)(2,1)}, bf16[3,198,256]{2,1,0:T(8,128)(2,1)}, u32[]{:S(2)}, u32[]{:S(2)}) collective-permute-start(bf16[3,198,256]{2,1,0:T(8,128)(2,1)} %slice.154), channel_id=1, source_target_pairs={{0,4},{4,8},{8,12},{12,16},{16,20},{20,24},{24,28},{1,5},{5,9},{9,... | collective-permute-start | bytes 912392 | tf_op jit(solution)/shard_map/ppermute | solution.py:227
  115.6 32.8 %copy-start.7 = (bf16[3,144,256]{2,1,0:T(8,128)(2,1)S(1)}, bf16[3,144,256]{2,1,0:T(8,128)(2,1)}, u32[]{:S(2)}) copy-start(bf16[3,144,256]{2,1,0:T(8,128)(2,1)} %copy-done.6) | copy-start | bytes 663556
  115.6 32.8 %copy-start.9 = (bf16[384,198]{1,0:T(8,128)(2,1)S(1)}, bf16[384,198]{1,0:T(8,128)(2,1)}, u32[]{:S(2)}) copy-start(bf16[384,198]{1,0:T(8,128)(2,1)} %constant.121.clone.refs_4_) | copy-start | bytes 456196
  115.6 32.8 %copy-start.10 = (bf16[384,144]{1,0:T(8,128)(2,1)S(1)}, bf16[384,144]{1,0:T(8,128)(2,1)}, u32[]{:S(2)}) copy-start(bf16[384,144]{1,0:T(8,128)(2,1)} %constant.122.clone.refs_5_) | copy-start | bytes 331780
  162.4 38.8 %all-to-all-start.5 = ((bf16[8,8,48,256]{3,2,1,0:T(8,128)(2,1)}), bf16[8,8,48,256]{3,2,1,0:T(8,128)(2,1)}, u32[]{:S(2)}, u32[]{:S(2)}) async-start(bf16[8,8,48,256]{3,2,1,0:T(8,128)(2,1)} %copy-done.5), calls=%async_computation.5 | async-start | bytes 3145728 | tf_op jit(solution)/shard_map/all_to_all | solution.py:284
  201.2 7.7 %copy-start.17 = (s32[64,64]{1,0:T(8,128)S(1)}, s32[64,64]{1,0:T(8,128)}, u32[]{:S(2)}) copy-start(s32[64,64]{1,0:T(8,128)} %param.12) | copy-start | bytes 49156
  201.2 42.3 %all-to-all-start.3 = ((bf16[8,8,48,256]{3,2,1,0:T(8,128)(2,1)}), bf16[8,8,48,256]{3,2,1,0:T(8,128)(2,1)}, u32[]{:S(2)}, u32[]{:S(2)}) async-start(bf16[8,8,48,256]{3,2,1,0:T(8,128)(2,1)} %copy-done.3), calls=%async_computation.3 | async-start | bytes 3145728 | tf_op jit(solution)/shard_map/all_to_all | solution.py:284
  243.5 42.1 %all-to-all-start.8 = ((bf16[8,8,48,256]{3,1,2,0:T(8,128)(2,1)}), bf16[8,8,48,256]{3,1,2,0:T(8,128)(2,1)}, u32[]{:S(2)}, u32[]{:S(2)}) async-start(bf16[8,8,48,256]{3,1,2,0:T(8,128)(2,1)} %copy.70), calls=%async_computation.8 | async-start | bytes 3145728 | tf_op jit(solution)/shard_map/all_to_all | solution.py:288
  285.6 42.1 %all-to-all-start.6 = ((bf16[8,8,48,256]{3,1,2,0:T(8,128)(2,1)}), bf16[8,8,48,256]{3,1,2,0:T(8,128)(2,1)}, u32[]{:S(2)}, u32[]{:S(2)}) async-start(bf16[8,8,48,256]{3,1,2,0:T(8,128)(2,1)} %copy.67), calls=%async_computation.6 | async-start | bytes 3145728 | tf_op jit(solution)/shard_map/all_to_all | solution.py:288
  327.7 42.2 %all-to-all-start.4 = ((bf16[8,8,48,256]{3,1,2,0:T(8,128)(2,1)}), bf16[8,8,48,256]{3,1,2,0:T(8,128)(2,1)}, u32[]{:S(2)}, u32[]{:S(2)}) async-start(bf16[8,8,48,256]{3,1,2,0:T(8,128)(2,1)} %copy.64), calls=%async_computation.4 | async-start | bytes 3145728 | tf_op jit(solution)/shard_map/all_to_all | solution.py:288
  (10 other events, 17.4 us)

commit v2 on v1

--- a/solution.py
+++ b/solution.py
@@ -57,7 +57,7 @@
     return (jnp.cos(angle_sum), jnp.sin(angle_sum))
 
 
-def lift_kernel(pieces, group, parents, targets, slots, octants, *refs):
+def lift_kernel(pieces, group, parents, slots, octants, *refs):
     blocks = refs[:pieces]
     ghosts = refs[pieces : 2 * pieces]
     weights = refs[2 * pieces : 3 * pieces]
@@ -96,15 +96,18 @@
 
     @pl.when(step == pl.num_programs(0) - 1)
     def _():
-        rows = send.shape[2]
-        for parent in range(parents):
-            values = total[parent].astype(out.dtype)
-            out[parent] = values
-            for target in range(targets):
-                send[target, parent] = values[target * rows : (target + 1) * rows]
-
-
-def lift(pieces, ghosts, weights, cosine, sine, slots, octants, parents, targets):
+        out[...] = total[...].astype(out.dtype)
+        tile = 8
+
+        @pl.loop(0, total.shape[1] // tile)
+        def _(index):
+            block = total[:, pl.ds(pl.multiple_of(index * tile, tile), tile), :]
+            block = jnp.swapaxes(block, 0, 1).reshape(tile * parents, block.shape[2])
+            span = pl.ds(pl.multiple_of(index * tile * parents, tile * parents), tile * parents)
+            send[span] = block.astype(send.dtype)
+
+
+def lift(pieces, ghosts, weights, cosine, sine, slots, octants, parents):
     children = pieces[0].shape[0]
     group = 8
     rows = weights[0].shape[0]
@@ -121,11 +124,11 @@
     in_specs += [whole(array) for array in (*ghosts, *weights, cosine, sine)]
     out_shape = [
         jax.ShapeDtypeStruct((parents, rows, width), jnp.bfloat16),
-        jax.ShapeDtypeStruct((targets, parents, rows // targets, width), jnp.bfloat16),
+        jax.ShapeDtypeStruct((rows * parents, width), jnp.bfloat16),
     ]
     flops = 2 * children * rows * width * sum(w.shape[1] for w in weights)
     return pl.pallas_call(
-        functools.partial(lift_kernel, count, group, parents, targets),
+        functools.partial(lift_kernel, count, group, parents),
         grid_spec=pltpu.PrefetchScalarGridSpec(
             num_scalar_prefetch=2,
             grid=(children // group,),
@@ -142,35 +145,124 @@
     )(slots, octants, *pieces, *ghosts, *weights, cosine, sine)
 
 
-def translate_kernel(operators, sources, out):
-    half = out.shape[-1] // 2
-    for index in range(out.shape[0]):
-        spectra = sources[index]
-        direct = jnp.dot(operators[0, index], spectra, preferred_element_type=jnp.float32)
-        cross = jnp.dot(operators[1, index], spectra, preferred_element_type=jnp.float32)
-        out[index, :, :half] = (direct[:, :half] - cross[:, half:]).astype(out.dtype)
-        out[index, :, half:] = (direct[:, half:] + cross[:, :half]).astype(out.dtype)
-
-
-def translate(operators, sources):
-    points, parents, width = sources.shape
-    group = next(size for size in (8, 6, 4, 3, 2, 1) if points % size == 0)
+def exchange_kernel(chunks, parents, ranks, *refs):
+    sent = refs[:chunks]
+    operators = refs[chunks : 2 * chunks]
+    out, held, ready, send_sem, recv_sem, own_sem = refs[2 * chunks :]
+    rows = held.shape[1] // chunks
+    width = held.shape[2]
+    half = width // 2
+    me = lax.axis_index("box")
+
+    barrier = pltpu.get_barrier_semaphore()
+    for offset in range(1, ranks):
+        pl.semaphore_signal(
+            barrier,
+            inc=1,
+            device_id={"box": lax.rem(me + offset, ranks)},
+            device_id_type=pl.DeviceIdType.MESH,
+        )
+    pl.semaphore_wait(barrier, ranks - 1)
+
+    def remote(phase, chunk, offset):
+        target = lax.rem(me + offset, ranks)
+        span = pl.ds(chunk * rows, rows)
+        source = sent[chunk].at[target] if phase == 0 else ready.at[target, span]
+        landing = held if phase == 0 else out
+        return pltpu.make_async_remote_copy(
+            src_ref=source,
+            dst_ref=landing.at[me, span],
+            send_sem=send_sem.at[phase, chunk, offset - 1],
+            recv_sem=recv_sem.at[phase, chunk, offset - 1],
+            device_id={"box": target},
+            device_id_type=pl.DeviceIdType.MESH,
+        )
+
+    def kept(phase, chunk):
+        span = pl.ds(chunk * rows, rows)
+        source = sent[chunk].at[me] if phase == 0 else ready.at[me, span]
+        landing = held if phase == 0 else out
+        return pltpu.make_async_copy(source, landing.at[me, span], own_sem.at[phase, chunk])
+
+    order = sorted(range(1, ranks), key=lambda offset: abs(offset - ranks / 2))
+    for chunk in range(chunks):
+        for offset in order:
+            remote(0, chunk, offset).start()
+        kept(0, chunk).start()
+
+    for chunk in range(chunks):
+        for offset in order:
+            remote(0, chunk, offset).wait_recv()
+        kept(0, chunk).wait()
+        table = operators[chunk]
+
+        @pl.loop(0, rows // (2 * parents))
+        def _(pair):
+            span = pl.ds(pl.multiple_of(chunk * rows + pair * 2 * parents, 16), 2 * parents)
+            both = [held[rank, span].astype(jnp.float32) for rank in range(ranks)]
+            results = []
+            for member in range(2):
+                low = member * parents
+                spectra = jnp.concatenate([value[low : low + parents] for value in both], axis=0)
+                spectra = spectra.astype(jnp.bfloat16)
+                product = jnp.dot(
+                    table[2 * pair + member], spectra, preferred_element_type=jnp.float32
+                )
+                count = product.shape[0] // 2
+                direct, cross = product[:count], product[count:]
+                results.append(
+                    jnp.concatenate(
+                        [
+                            direct[:, :half] - cross[:, half:],
+                            direct[:, half:] + cross[:, :half],
+                        ],
+                        axis=1,
+                    )
+                )
+            for rank in range(ranks):
+                low = rank * parents
+                value = jnp.concatenate(
+                    [result[low : low + parents] for result in results], axis=0
+                )
+                ready[rank, span] = value.astype(jnp.bfloat16)
+
+        for offset in order:
+            remote(1, chunk, offset).start()
+        kept(1, chunk).start()
+
+    for chunk in range(chunks):
+        for offset in order:
+            remote(1, chunk, offset).wait_recv()
+        kept(1, chunk).wait()
+    for phase in range(2):
+        for chunk in range(chunks):
+            for offset in order:
+                remote(phase, chunk, offset).wait_send()
+
+
+def exchange(sent, operators, parents):
+    chunks = len(sent)
+    ranks, rows, width = sent[0].shape
+    whole = (ranks, chunks * rows, width)
+    in_specs = [pl.BlockSpec(memory_space=pl.ANY)] * chunks
+    in_specs += [pl.BlockSpec(memory_space=pltpu.VMEM)] * chunks
     return pl.pallas_call(
-        translate_kernel,
-        grid=(points // group,),
-        in_specs=[
-            pl.BlockSpec((2, group, parents, parents), lambda step: (0, step, 0, 0)),
-            pl.BlockSpec((group, parents, width), lambda step: (step, 0, 0)),
+        functools.partial(exchange_kernel, chunks, parents, ranks),
+        in_specs=in_specs,
+        out_specs=pl.BlockSpec(memory_space=pl.ANY),
+        out_shape=jax.ShapeDtypeStruct(whole, jnp.bfloat16),
+        scratch_shapes=[
+            pltpu.VMEM(whole, jnp.bfloat16),
+            pltpu.VMEM(whole, jnp.bfloat16),
+            pltpu.SemaphoreType.DMA((2, chunks, ranks - 1)),
+            pltpu.SemaphoreType.DMA((2, chunks, ranks - 1)),
+            pltpu.SemaphoreType.DMA((2, chunks)),
         ],
-        out_specs=pl.BlockSpec((group, parents, width), lambda step: (step, 0, 0)),
-        out_shape=jax.ShapeDtypeStruct(sources.shape, jnp.bfloat16),
-        cost_estimate=pl.CostEstimate(
-            flops=16 * points * parents * parents * width,
-            bytes_accessed=8 * sources.size,
-            transcendentals=0,
+        compiler_params=pltpu.CompilerParams(
+            collective_id=0, has_side_effects=True, vmem_limit_bytes=40 * 2**20
         ),
-        name="translate",
-    )(operators, sources)
+        name="exchange",
+    )(*sent, *operators)
 
 
 def shared_out(block, ways):
@@ -248,6 +340,9 @@
     operators = jnp.dot(own, chosen.astype(jnp.bfloat16), preferred_element_type=jnp.float32)
     operators = operators.astype(jnp.bfloat16)
     operators = operators.reshape(2, chunks, points, parents_all, parents_all)
+    operators = operators.transpose(1, 2, 0, 3, 4)
+    operators = operators.reshape(chunks, points, 2 * parents_all, parents_all)
+    own_shape = (parents, theta_fine, local_fine, width)
 
     own_parts, sent_parts = [], []
     for chunk in range(chunks):
@@ -274,21 +369,14 @@
             slots,
             octants,
             parents,
-            rows,
         )
         own_parts.append(part.reshape(parents, fine_chunk, local_fine, width))
-        sent_parts.append(sent)
-
-    results = []
-    for chunk in range(chunks):
-        got = lax.all_to_all(sent_parts[chunk], "box", split_axis=0, concat_axis=0, tiled=True)
-        got = got.reshape(parents_all, points, width).transpose(1, 0, 2)
-        moved = translate(operators[:, chunk], got).transpose(1, 0, 2)
-        moved = moved.reshape(rows, parents, points, width)
-        back = lax.all_to_all(moved, "box", split_axis=0, concat_axis=0, tiled=True)
-        back = back.transpose(1, 0, 2, 3)
-        results.append(back.reshape(parents, fine_chunk, local_fine, width))
-    return jnp.concatenate(own_parts, axis=1), jnp.concatenate(results, axis=1)
+        sent_parts.append(sent.reshape(rows, points * parents, width))
+
+    incoming = exchange(sent_parts, [operators[chunk] for chunk in range(chunks)], parents)
+    incoming = incoming.reshape(rows, chunks, theta_local, local_fine, parents, width)
+    incoming = incoming.transpose(4, 1, 0, 2, 3, 5).reshape(own_shape)
+    return jnp.concatenate(own_parts, axis=1), incoming
 
 
 def solution(mesh):

time: 380 us -> 372 us (0.979); the launches traced: 374 us -> 372 us
  Pallas kernels: 49.8 us -> 244 us
  waiting for transfers between devices: 159 us -> 35.4 us
  starting transfers between devices: 63.1 us -> 23.8 us
  local copies, waits for them, and re-layouts: 83.8 us -> 57.1 us
  other arithmetic: 14.1 us -> 8.92 us
    pallas_call x6 -> x4, Pallas kernels: 49.8 us -> 244 us  [the longest x1 209 us: exchange(): pl.pallas_call(functools.partial(exchange_kernel, chunks, parents, ranks)...]
    all_to_all x6 -> x0, waiting for transfers between devices: 100 us -> none  [the longest x3 72.7 us: local(): back = lax.all_to_all(moved, 'box', split_axis=0, concat_axis=0, tiled=True)]
    all_to_all x6 -> x0, starting transfers between devices: 39.9 us -> none  [the longest x3 22.7 us: local(): back = lax.all_to_all(moved, 'box', split_axis=0, concat_axis=0, tiled=True)]
    ppermute x3, waiting for transfers between devices: 33.3 us -> 0.01 us  [local(): ghosts.append(lax.ppermute(got[-straddle:], 'box', forward))]
    reshape x6 -> x0, local copies, waits for them, and re-layouts: 14.5 us -> none  [the longest x3 8.04 us: local(): moved = moved.reshape(rows, parents, points, width)]
    all_to_all x3, waiting for transfers between devices: 25.8 us -> 35.4 us  [local(): got = lax.all_to_all(sent, 'dir', split_axis=0, concat_axis=0, tiled=True)]
    all_to_all x3 -> x0, local copies, waits for them, and re-layouts: 9.25 us -> none  [local(): lax.all_to_all(sent_parts[chunk], 'box', split_axis=0, concat_axis=0, til...]
    squeeze x1 -> x0, local copies, waits for them, and re-layouts: 4.91 us -> none  [local(): moved = translate(operators[:, chunk], got).transpose(1, 0, 2)]
  transfers between devices with their start and end apart: 13 -> 7, of which waited for: 10 -> 3; matrix products, arithmetic and copies ran while one was open for 22% -> 11% of each run, Pallas kernels for 13% -> 3%
where the time goes in v2:
time: 372 us
  Pallas kernels  244 us (66%)
  local copies, waits for them, and re-layouts  57.1 us (15%)
  waiting for transfers between devices  35.4 us (10%)
  starting transfers between devices  23.8 us (6%)
  other arithmetic  8.92 us (2%)
    pallas_call x1, Pallas kernels, exchange(): pl.pallas_call(functools.partial(exchange_kernel, chunks, parents, ranks)...  209 us
    pallas_call x3, Pallas kernels, lift(): pl.pallas_call(functools.partial(lift_kernel, count, group, parents), gri...  35.5 us
    all_to_all x3, waiting for transfers between devices, local(): got = lax.all_to_all(sent, 'dir', split_axis=0, concat_axis=0, tiled=True)  35.4 us
    all_to_all x3, starting transfers between devices, local(): got = lax.all_to_all(sent, 'dir', split_axis=0, concat_axis=0, tiled=True)  13.8 us
    broadcast_in_dim x12, local copies, waits for them, and re-layouts, lanes(): return jnp.broadcast_to(part, part.shape[:2] + (width // 2,))  11.5 us
    unnamed x67, local copies, waits for them, and re-layouts  11.4 us
    reshape x2, local copies, waits for them, and re-layouts, local(): operators = operators.reshape(2, chunks, points, parents_all, parents_all)  9.49 us
    ppermute x3, starting transfers between devices, local(): ghosts.append(lax.ppermute(got[-straddle:], 'box', forward))  8.02 us
  transfers between devices with their start and end apart: 7, of which 3 were waited for; matrix products, arithmetic and copies ran while one was open for 11% of the time, Pallas kernels for 3%

profile of v2, /device:TPU:16, one launch (start us, length us, event | category | flops | bytes accessed | tf_op | source)
XLA Modules:
  0.0 372.2 jit_solution(2885219440308696827)
XLA Ops:
  5.7 4.4 %all-to-all-start.2 = ((bf16[4,8,90,256]{3,1,2,0:T(8,128)(2,1)}), bf16[4,8,90,256]{3,1,2,0:T(8,128)(2,1)}, u32[]{:S(2)}, u32[]{:S(2)}) async-start(bf16[4,8,90,256]{3,1,2,0:T(8,128)(2,1)} %pad_maximum_fusion.3), calls=%async_computation.2 | async-start | bytes 2949120 | tf_op jit(solution)/shard_map/all_to_all | solution.py:316
  10.1 2.8 slice-done.1
  17.4 11.2 %all-to-all-done.2 = bf16[4,8,90,256]{3,1,2,0:T(8,128)(2,1)} async-done(((bf16[4,8,90,256]{3,1,2,0:T(8,128)(2,1)}), bf16[4,8,90,256]{3,1,2,0:T(8,128)(2,1)}, u32[]{:S(2)}, u32[]{:S(2)}) %all-to-all-start.2) | async-done | bytes 1474592 | tf_op jit(solution)/shard_map/all_to_all | solution.py:316
  28.6 4.5 %all-to-all-start.1 = ((bf16[4,8,144,256]{3,1,2,0:T(8,128)(2,1)}), bf16[4,8,144,256]{3,1,2,0:T(8,128)(2,1)}, u32[]{:S(2)}, u32[]{:S(2)}) async-start(bf16[4,8,144,256]{3,1,2,0:T(8,128)(2,1)} %pad_maximum_fusion.2), calls=%async_computation.1 | async-start | bytes 4718592 | tf_op jit(solution)/shard_map/all_to_all | solution.py:316
  33.2 2.0 collective-permute-start
  37.5 3.1 fusion.20
  41.2 1.9 pad_maximum_fusion.1
  43.1 17.2 %all-to-all-done.1 = bf16[4,8,144,256]{3,1,2,0:T(8,128)(2,1)} async-done(((bf16[4,8,144,256]{3,1,2,0:T(8,128)(2,1)}), bf16[4,8,144,256]{3,1,2,0:T(8,128)(2,1)}, u32[]{:S(2)}, u32[]{:S(2)}) %all-to-all-start.1) | async-done | bytes 2359328 | tf_op jit(solution)/shard_map/all_to_all | solution.py:316
  60.4 4.9 %all-to-all-start = ((bf16[4,8,198,256]{3,1,2,0:T(8,128)(2,1)}), bf16[4,8,198,256]{3,1,2,0:T(8,128)(2,1)}, u32[]{:S(2)}, u32[]{:S(2)}) async-start(bf16[4,8,198,256]{3,1,2,0:T(8,128)(2,1)} %pad_maximum_fusion.1), calls=%async_computation | async-start | bytes 6488064 | tf_op jit(solution)/shard_map/all_to_all | solution.py:316
  70.8 6.1 %reshape.279 = bf16[2,3,48,64,64]{4,3,2,1,0:T(8,128)(2,1)} reshape(bf16[288,4096]{1,0:T(8,128)(2,1)S(1)} %convolution_convert_fusion) | data formatting | bytes 4718592 | tf_op jit(solution)/shard_map/reshape | solution.py:342
  76.8 3.4 copy.49
  80.3 2.3 fusion.18
  86.3 1.9 collective-permute-start.3
  88.2 2.1 copy.24
  91.1 3.6 collective-permute-start.2
  94.8 7.0 %all-to-all-done = bf16[4,8,198,256]{3,1,2,0:T(8,128)(2,1)} async-done(((bf16[4,8,198,256]{3,1,2,0:T(8,128)(2,1)}), bf16[4,8,198,256]{3,1,2,0:T(8,128)(2,1)}, u32[]{:S(2)}, u32[]{:S(2)}) %all-to-all-start) | async-done | bytes 3244064 | tf_op jit(solution)/shard_map/all_to_all | solution.py:316
  101.7 2.6 copy.18
  104.4 2.5 collective-permute-start.1
  110.3 12.4 %lift.5 = (bf16[8,384,256]{2,1,0:T(8,128)(2,1)S(1)}, bf16[3072,256]{1,0:T(8,128)(2,1)S(1)}) custom-call(s32[35]{0:T(128)S(1)} %fusion.13.slots, s32[35]{0:T(128)S(1)} %get-tuple-element.14.octants, bf16[32,144,256]{2,1,0:T(8,128)(2,1)} %bitcast.61, bf16[32,90,256]{2,1,0:T(8,128)(2,1)S(1)} %bitcast.44, ...), custom_call_target="tpu_custom_call" | custom-call | flops 5888802816 | bytes 3833856 | tf_op jit(solution)/shard_map/lift/pallas_call | solution.py:130
  124.8 10.8 %lift.3 = (bf16[8,384,256]{2,1,0:T(8,128)(2,1)S(1)}, bf16[3072,256]{1,0:T(8,128)(2,1)S(1)}) custom-call(s32[35]{0:T(128)S(1)} %fusion.13.slots, s32[35]{0:T(128)S(1)} %get-tuple-element.14.octants, bf16[32,198,256]{2,1,0:T(8,128)(2,1)} %bitcast.54, bf16[3,198,256]{2,1,0:T(8,128)(2,1)S(1)} %collective-permute-done.1.refs_1_.refs_2_, ...), custom_call_target="tpu_custom_call" | custom-call | flops 4982833152 | bytes 3244032 | tf_op jit(solution)/shard_map/lift/pallas_call | solution.py:130
  140.3 12.4 %lift.4 = (bf16[8,384,256]{2,1,0:T(8,128)(2,1)S(1)}, bf16[3072,256]{1,0:T(8,128)(2,1)S(1)}) custom-call(s32[35]{0:T(128)S(1)} %fusion.13.slots, s32[35]{0:T(128)S(1)} %get-tuple-element.14.octants, bf16[32,198,256]{2,1,0:T(8,128)(2,1)} %bitcast.55, bf16[32,144,256]{2,1,0:T(8,128)(2,1)} %bitcast.62, ...), custom_call_target="tpu_custom_call" | custom-call | flops 8606711808 | bytes 5603328 | tf_op jit(solution)/shard_map/lift/pallas_call | solution.py:130
  157.8 208.7 %exchange.1 = bf16[8,1152,256]{2,1,0:T(8,128)(2,1)S(1)} custom-call(bf16[8,384,256]{2,1,0:T(8,128)(2,1)S(1)} %bitcast.48, bf16[8,384,256]{2,1,0:T(8,128)(2,1)S(1)} %bitcast.50, bf16[8,384,256]{2,1,0:T(8,128)(2,1)S(1)} %bitcast.46, bf16[48,128,64]{2,1,0:T(8,128)(2,1)S(1)} %bitcast.42, bf16[48,128,64]{2,1,0:T(8,128)(2,1)S(1)} %bitcast.41, ...), custom_call_target="tpu_custom_call" | custom-call | tf_op jit(solution)/shard_map/exchange/pallas_call | solution.py:249
  366.5 3.2 copy.32
  369.7 2.4 pad_maximum_fusion
  (120 shorter events, 37.7 us)
Async XLA Ops:
  0.6 68.6 %copy-start = (bf16[2,316,48,24]{1,3,2,0:T(8,128)(2,1)S(1)}, bf16[2,316,48,24]{1,3,2,0:T(8,128)(2,1)}, u32[]{:S(2)}) copy-start(bf16[2,316,48,24]{1,3,2,0:T(8,128)(2,1)} %param.11) | copy-start | bytes 4368388
  5.7 22.9 %all-to-all-start.2 = ((bf16[4,8,90,256]{3,1,2,0:T(8,128)(2,1)}), bf16[4,8,90,256]{3,1,2,0:T(8,128)(2,1)}, u32[]{:S(2)}, u32[]{:S(2)}) async-start(bf16[4,8,90,256]{3,1,2,0:T(8,128)(2,1)} %pad_maximum_fusion.3), calls=%async_computation.2 | async-start | bytes 2949120 | tf_op jit(solution)/shard_map/all_to_all | solution.py:316
  10.1 3.7 copy-start.17
  17.4 15.7 %copy-start.25 = (s32[32]{0:T(128)S(1)}, s32[32]{0:T(128)}, u32[]{:S(2)}) copy-start(s32[32]{0:T(128)} %param.10) | copy-start | bytes 388
  28.6 31.8 %all-to-all-start.1 = ((bf16[4,8,144,256]{3,1,2,0:T(8,128)(2,1)}), bf16[4,8,144,256]{3,1,2,0:T(8,128)(2,1)}, u32[]{:S(2)}, u32[]{:S(2)}) async-start(bf16[4,8,144,256]{3,1,2,0:T(8,128)(2,1)} %pad_maximum_fusion.2), calls=%async_computation.1 | async-start | bytes 4718592 | tf_op jit(solution)/shard_map/all_to_all | solution.py:316
  33.2 49.3 %collective-permute-start = (s32[3]{0:T(128)S(1)}, s32[3]{0:T(128)S(1)}, u32[]{:S(2)}, u32[]{:S(2)}) collective-permute-start(s32[3]{0:T(128)S(1)} %slice.123), channel_id=1, source_target_pairs={{0,4},{4,8},{8,12},{12,16},{16,20},{20,24},{24,28},{1,5},{5,9},{9,... | collective-permute-start | bytes 44 | tf_op jit(solution)/shard_map/ppermute | solution.py:307
  43.1 26.0 %copy-start.24 = (s32[64,64]{1,0:T(8,128)S(1)}, s32[64,64]{1,0:T(8,128)}, u32[]{:S(2)}) copy-start(s32[64,64]{1,0:T(8,128)} %param.12) | copy-start | bytes 49156
  60.4 41.4 %all-to-all-start = ((bf16[4,8,198,256]{3,1,2,0:T(8,128)(2,1)}), bf16[4,8,198,256]{3,1,2,0:T(8,128)(2,1)}, u32[]{:S(2)}, u32[]{:S(2)}) async-start(bf16[4,8,198,256]{3,1,2,0:T(8,128)(2,1)} %pad_maximum_fusion.1), calls=%async_computation | async-start | bytes 6488064 | tf_op jit(solution)/shard_map/all_to_all | solution.py:316
  86.3 20.7 %collective-permute-start.3 = (bf16[3,90,256]{2,1,0:T(8,128)(2,1)}, bf16[3,90,256]{2,1,0:T(8,128)(2,1)S(1)}, u32[]{:S(2)}, u32[]{:S(2)}) collective-permute-start(bf16[3,90,256]{2,1,0:T(8,128)(2,1)} %slice.163), channel_id=1, source_target_pairs={{0,4},{4,8},{8,12},{12,16},{16,20},{20,24},{24,28},{1,5},{5,9},{9,... | collective-permute-start | bytes 414728 | tf_op jit(solution)/shard_map/ppermute | solution.py:319
  90.3 4.3 %copy-start.19 = (bf16[4,8,144,256]{3,2,1,0:T(8,128)(2,1)}, bf16[4,8,144,256]{3,2,1,0:T(8,128)(2,1)S(1)}, u32[]{:S(2)}) copy-start(bf16[4,8,144,256]{3,2,1,0:T(8,128)(2,1)S(1)} %copy.24) | copy-start | bytes 7077892
  91.1 15.9 %collective-permute-start.2 = (bf16[3,144,256]{2,1,0:T(8,128)(2,1)}, bf16[3,144,256]{2,1,0:T(8,128)(2,1)S(1)}, u32[]{:S(2)}, u32[]{:S(2)}) collective-permute-start(bf16[3,144,256]{2,1,0:T(8,128)(2,1)} %slice.160), channel_id=1, source_target_pairs={{0,4},{4,8},{8,12},{12,16},{16,20},{20,24},{24,28},{1,5},{5,9},{9,... | collective-permute-start | bytes 663560 | tf_op jit(solution)/shard_map/ppermute | solution.py:319
  101.7 5.2 %copy-start.22 = (f32[8,384]{1,0:T(8,128)S(1)}, f32[8,384]{1,0:T(8,128)}, u32[]{:S(2)}) copy-start(f32[8,384]{1,0:T(8,128)} %broadcast_in_dim.63) | copy-start | bytes 36868
  104.3 18.3 %copy-start.18 = (bf16[4,8,198,256]{3,2,1,0:T(8,128)(2,1)}, bf16[4,8,198,256]{3,2,1,0:T(8,128)(2,1)S(1)}, u32[]{:S(2)}) copy-start(bf16[4,8,198,256]{3,2,1,0:T(8,128)(2,1)S(1)} %copy.18) | copy-start | bytes 9732100
  104.3 4.3 %copy-start.23 = (f32[8,384]{1,0:T(8,128)S(1)}, f32[8,384]{1,0:T(8,128)}, u32[]{:S(2)}) copy-start(f32[8,384]{1,0:T(8,128)} %broadcast_in_dim.65) | copy-start | bytes 36868
  104.3 5.9 %copy-start.4 = (bf16[4,8,90,256]{3,2,1,0:T(8,128)(2,1)S(1)}, bf16[4,8,90,256]{3,2,1,0:T(8,128)(2,1)}, u32[]{:S(2)}) copy-start(bf16[4,8,90,256]{3,2,1,0:T(8,128)(2,1)} %copy-done.3) | copy-start | bytes 4423684
  104.3 5.9 %copy-start.15 = (bf16[384,144]{1,0:T(8,128)(2,1)S(1)}, bf16[384,144]{1,0:T(8,128)(2,1)}, u32[]{:S(2)}) copy-start(bf16[384,144]{1,0:T(8,128)(2,1)} %constant.123.clone.refs_4_) | copy-start | bytes 331780
  104.3 5.9 %copy-start.16 = (bf16[384,90]{1,0:T(8,128)(2,1)S(1)}, bf16[384,90]{1,0:T(8,128)(2,1)}, u32[]{:S(2)}) copy-start(bf16[384,90]{1,0:T(8,128)(2,1)} %constant.124.clone.refs_5_) | copy-start | bytes 207364
  104.4 18.3 %collective-permute-start.1 = (bf16[3,198,256]{2,1,0:T(8,128)(2,1)S(1)}, bf16[3,198,256]{2,1,0:T(8,128)(2,1)S(1)}, u32[]{:S(2)}, u32[]{:S(2)}) collective-permute-start(bf16[3,198,256]{2,1,0:T(8,128)(2,1)S(1)} %slice.157), channel_id=1, source_target_pairs={{0,4},{4,8},{8,12},{12,16},{16,20},{20,24},{24,28},{1,5},{5,9},{9,... | collective-permute-start | bytes 912392 | tf_op jit(solution)/shard_map/ppermute | solution.py:319
  110.2 12.4 %copy-start.20 = (f32[8,384]{1,0:T(8,128)S(1)}, f32[8,384]{1,0:T(8,128)}, u32[]{:S(2)}) copy-start(f32[8,384]{1,0:T(8,128)} %broadcast_in_dim.55) | copy-start | bytes 36868
  110.2 12.9 %copy-start.21 = (f32[8,384]{1,0:T(8,128)S(1)}, f32[8,384]{1,0:T(8,128)}, u32[]{:S(2)}) copy-start(f32[8,384]{1,0:T(8,128)} %broadcast_in_dim.57) | copy-start | bytes 36868
  135.5 3.3 copy-start.12
  135.6 3.3 copy-start.13
  140.3 14.7 %copy-start.2 = (bf16[1,48,2,64,64]{4,3,2,1,0:T(8,128)(2,1)S(1)}, bf16[1,48,2,64,64]{4,3,2,1,0:T(8,128)(2,1)}, u32[]{:S(2)}) copy-start(bf16[1,48,2,64,64]{4,3,2,1,0:T(8,128)(2,1)} %get-tuple-element.18) | copy-start | bytes 2359300
  366.5 3.3 copy-start.8
  (12 other events, 22.0 us)

commit v3 on v2

v3 whole, which is shorter than its diff:
```python
import functools

import jax
import jax.numpy as jnp
import ml_dtypes
import numpy as np
from jax import lax
from jax.experimental import pallas as pl
from jax.experimental.pallas import tpu as pltpu
from jax.sharding import PartitionSpec as P

wave_shift = 5.0
midpoint_taps = (3.0, -25.0, 150.0, 150.0, -25.0, 3.0)
halo = 3
straddle = 3


def theta_table(coarse_count):
    fine_count = 2 * coarse_count
    table_rows = np.zeros((fine_count, coarse_count))
    for target in range(fine_count):
        position = target / 2.0 - 0.25
        window_start = min(max(int(np.floor(position)) - 2, 0), coarse_count - 6)
        for tap_index in range(6):
            weight_value = 1.0
            for other_tap in range(6):
                if other_tap != tap_index:
                    weight_value *= (position - window_start - other_tap) / (tap_index - other_tap)
            table_rows[target, window_start + tap_index] = weight_value
    return table_rows


def local_phi_table(local_count):
    table_rows = np.zeros((2 * local_count, local_count + 2 * halo))
    for target in range(2 * local_count):
        if target % 2 == 0:
            table_rows[target, target // 2 + halo] = 1.0
        else:
            middle = (target - 1) // 2
            for offset in range(6):
                table_rows[target, middle + 1 + offset] = midpoint_taps[offset] / 256.0
    return table_rows


def phase_factors(octants, theta_count, phi_angles):
    theta_angles = jnp.pi * (jnp.arange(theta_count, dtype=jnp.float32) + 0.5) / theta_count
    sign_x = ((octants % 2).astype(jnp.float32) * 2.0 - 1.0)[:, None, None]
    sign_y = ((octants // 2 % 2).astype(jnp.float32) * 2.0 - 1.0)[:, None, None]
    sign_z = ((octants // 4).astype(jnp.float32) * 2.0 - 1.0)[:, None, None]
    sine_theta = jnp.sin(theta_angles)[None, :, None]
    cosine_theta = jnp.cos(theta_angles)[None, :, None]
    angle_sum = wave_shift * (
        sign_x * sine_theta * jnp.cos(phi_angles)[None, None, :]
        + sign_y * sine_theta * jnp.sin(phi_angles)[None, None, :]
        + sign_z * cosine_theta
    )
    return (jnp.cos(angle_sum), jnp.sin(angle_sum))


def spectra_kernel(chunks, parents, ranks, ways, plan, *refs):
    first, packed, refs = refs[0], refs[1:chunks], refs[chunks:]
    keeps, octants, signs, lasts, refs = *refs[:4], refs[4:]
    used = sum(len(pieces) for pieces in plan)
    flat_weights, refs = refs[:used], refs[used:]
    cosine, sine, refs = refs[:chunks], refs[chunks : 2 * chunks], refs[2 * chunks :]
    operators, refs = refs[:chunks], refs[chunks:]
    own_out, out, refs = refs[0], refs[1], refs[2:]
    columns, refs = refs[:chunks], refs[chunks:]
    running, staged, sent, held, ready = refs[:5]
    dir_send, dir_recv, ghost_send, ghost_recv, keep_sem, box_send, box_recv, own_sem = refs[5:]
    weights = []
    for pieces in plan:
        weights.append(flat_weights[: len(pieces)])
        flat_weights = flat_weights[len(pieces) :]

    rows = held.shape[1] // chunks
    points = running.shape[1]
    width = held.shape[2]
    half = width // 2
    children = columns[0].shape[0]
    share = (children - straddle) // ways
    me = lax.axis_index("box")
    side = lax.axis_index("dir")

    def to_box(target):
        return dict(device_id={"box": target}, device_id_type=pl.DeviceIdType.MESH)

    def to_dir(target):
        return dict(device_id={"dir": target}, device_id_type=pl.DeviceIdType.MESH)

    barrier = pltpu.get_barrier_semaphore()
    for offset in range(1, ranks):
        pl.semaphore_signal(barrier, inc=1, **to_box(lax.rem(me + offset, ranks)))
    for offset in range(1, ways):
        pl.semaphore_signal(barrier, inc=1, **to_dir(lax.rem(side + offset, ways)))
    pl.semaphore_wait(barrier, ranks + ways - 2)

    def dir_copy(piece, offset):
        target = lax.rem(side + offset, ways)
        return pltpu.make_async_remote_copy(
            src_ref=packed[piece - 1].at[target],
            dst_ref=columns[piece].at[pl.ds(straddle + side * share, share)],
            send_sem=dir_send.at[piece - 1, offset - 1],
            recv_sem=dir_recv.at[piece - 1, offset - 1],
            **to_dir(target),
        )

    def dir_kept(piece):
        if piece == 0:
            source, landing = first, columns[0].at[pl.ds(straddle, children - straddle)]
        else:
            source = packed[piece - 1].at[side]
            landing = columns[piece].at[pl.ds(straddle + side * share, share)]
        return pltpu.make_async_copy(source, landing, keep_sem.at[piece])

    def ghost_copy(piece):
        if piece == 0:
            source = first.at[pl.ds(children - 2 * straddle, straddle)]
        else:
            source = columns[piece].at[pl.ds(children - straddle, straddle)]
        return pltpu.make_async_remote_copy(
            src_ref=source,
            dst_ref=columns[piece].at[pl.ds(0, straddle)],
            send_sem=ghost_send.at[piece],
            recv_sem=ghost_recv.at[piece],
            **to_box(me + 1),
        )

    def box_copy(phase, chunk, offset):
        target = lax.rem(me + offset, ranks)
        span = pl.ds(chunk * rows, rows)
        if phase == 0:
            source = sent.at[chunk, pl.ds(pl.multiple_of(target * rows, 16), rows)]
        else:
            source = ready.at[target, span]
        landing = held if phase == 0 else out
        return pltpu.make_async_remote_copy(
            src_ref=source,
            dst_ref=landing.at[me, span],
            send_sem=box_send.at[phase, chunk, offset - 1],
            recv_sem=box_recv.at[phase, chunk, offset - 1],
            **to_box(target),
        )

    def box_kept(phase, chunk):
        span = pl.ds(chunk * rows, rows)
        if phase == 0:
            source = sent.at[chunk, pl.ds(pl.multiple_of(me * rows, 16), rows)]
        else:
            source = ready.at[me, span]
        landing = held if phase == 0 else out
        return pltpu.make_async_copy(source, landing.at[me, span], own_sem.at[phase, chunk])

    def own_copy(chunk):
        return pltpu.make_async_copy(
            staged.at[chunk], own_out.at[:, pl.ds(chunk * points, points)], own_sem.at[2, chunk]
        )

    order = sorted(range(1, ranks), key=lambda offset: abs(offset - ranks / 2))

    def forward_ghosts(piece):
        @pl.when(me < ranks - 1)
        def _():
            ghost_copy(piece).start()

    def await_ghosts(piece):
        @pl.when(me > 0)
        def _():
            ghost_copy(piece).wait_recv()

    forward_ghosts(0)
    dir_kept(0).start()
    for piece in range(1, chunks):
        for offset in range(1, ways):
            dir_copy(piece, offset).start()
        dir_kept(piece).start()

    @pl.when(me == 0)
    def _():
        for piece in range(chunks):
            columns[piece][0:straddle] = jnp.zeros((straddle,) + columns[piece].shape[1:], jnp.bfloat16)

    running[0] = jnp.zeros(running.shape[1:], jnp.float32)

    for chunk in range(chunks):
        dir_kept(chunk).wait()
        if chunk > 0:
            for offset in range(1, ways):
                dir_copy(chunk, offset).wait_recv()
            forward_ghosts(chunk)
        await_ghosts(chunk)

        @pl.loop(0, children)
        def _(child):
            lifted = None
            for piece, weight in zip(plan[chunk], weights[chunk]):
                part = jnp.dot(
                    weight[...], columns[piece][child], preferred_element_type=jnp.float32
                )
                lifted = part if lifted is None else lifted + part
            octant = octants[child]
            keep = keeps[child]
            turn_cos = cosine[chunk][octant]
            turn_sin = sine[chunk][octant] * signs[child]
            real_part = lifted[:, :half]
            imag_part = lifted[:, half:]
            running[child + 1, :, :half] = (
                keep * running[child, :, :half] + turn_cos * real_part - turn_sin * imag_part
            )
            running[child + 1, :, half:] = (
                keep * running[child, :, half:] + turn_sin * real_part + turn_cos * imag_part
            )

        @pl.loop(0, points // 16)
        def _(tile):
            span = pl.ds(pl.multiple_of(tile * 16, 16), 16)
            values = [running[lasts[parent], span, :] for parent in range(parents)]
            for parent in range(parents):
                staged[chunk, parent, span] = values[parent].astype(jnp.bfloat16)
            for part in range(2):
                block = jnp.stack([value[8 * part : 8 * part + 8] for value in values])
                block = jnp.swapaxes(block, 0, 1).reshape(8 * parents, width)
                low = pl.multiple_of((2 * tile + part) * 8 * parents, 8 * parents)
                sent[chunk, pl.ds(low, 8 * parents)] = block.astype(jnp.bfloat16)

        for offset in order:
            box_copy(0, chunk, offset).start()
        box_kept(0, chunk).start()
        own_copy(chunk).start()

    for chunk in range(chunks):
        for offset in order:
            box_copy(0, chunk, offset).wait_recv()
        box_kept(0, chunk).wait()
        table = operators[chunk]

        @pl.loop(0, rows // (2 * parents))
        def _(pair):
            span = pl.ds(pl.multiple_of(chunk * rows + pair * 2 * parents, 16), 2 * parents)
            both = [held[rank, span].astype(jnp.float32) for rank in range(ranks)]
            results = []
            for member in range(2):
                low = member * parents
                spectra = jnp.concatenate([value[low : low + parents] for value in both], axis=0)
                spectra = spectra.astype(jnp.bfloat16)
                product = jnp.dot(
                    table[2 * pair + member], spectra, preferred_element_type=jnp.float32
                )
                count = product.shape[0] // 2
                direct, cross = product[:count], product[count:]
                results.append(
                    jnp.concatenate(
                        [
                            direct[:, :half] - cross[:, half:],
                            direct[:, half:] + cross[:, :half],
                        ],
                        axis=1,
                    )
                )
            for rank in range(ranks):
                low = rank * parents
                value = jnp.concatenate(
                    [result[low : low + parents] for result in results], axis=0
                )
                ready[rank, span] = value.astype(jnp.bfloat16)

        for offset in order:
            box_copy(1, chunk, offset).start()
        box_kept(1, chunk).start()

    for chunk in range(chunks):
        for offset in order:
            box_copy(1, chunk, offset).wait_recv()
        box_kept(1, chunk).wait()
        own_copy(chunk).wait()

        @pl.when(me < ranks - 1)
        def _():
            ghost_copy(chunk).wait_send()

        if chunk > 0:
            for offset in range(1, ways):
                dir_copy(chunk, offset).wait_send()
        for phase in range(2):
            for offset in order:
                box_copy(phase, chunk, offset).wait_send()


def spectra(first, packed, scalars, plan, weights, cosine, sine, operators, parents, ranks):
    chunks = len(plan)
    ways = packed[0].shape[0]
    children = first.shape[0] + straddle
    width = first.shape[-1]
    points = weights[0][0].shape[0]
    rows = points * parents // ranks
    whole = (ranks, chunks * rows, width)
    arrays = [first, *packed, *scalars, *sum(weights, []), *cosine, *sine, *operators]
    in_specs = [pl.BlockSpec(memory_space=pl.ANY)] * chunks
    in_specs += [pl.BlockSpec(memory_space=pltpu.SMEM)] * len(scalars)
    in_specs += [pl.BlockSpec(memory_space=pltpu.VMEM)] * (len(arrays) - len(in_specs))
    piece_rows = [first.shape[1]] + [piece.shape[2] for piece in packed]
    dma = pltpu.SemaphoreType.DMA
    return pl.pallas_call(
        functools.partial(spectra_kernel, chunks, parents, ranks, ways, plan),
        in_specs=in_specs,
        out_specs=[pl.BlockSpec(memory_space=pl.ANY)] * 2,
        out_shape=[
            jax.ShapeDtypeStruct((parents, chunks * points, width), jnp.bfloat16),
            jax.ShapeDtypeStruct(whole, jnp.bfloat16),
        ],
        scratch_shapes=[
            *[pltpu.VMEM((children, count, width), jnp.bfloat16) for count in piece_rows],
            pltpu.VMEM((children + 1, points, width), jnp.float32),
            pltpu.VMEM((chunks, parents, points, width), jnp.bfloat16),
            pltpu.VMEM((chunks, ranks * rows, width), jnp.bfloat16),
            pltpu.VMEM(whole, jnp.bfloat16),
            pltpu.VMEM(whole, jnp.bfloat16),
            dma((chunks - 1, ways - 1)),
            dma((chunks - 1, ways - 1)),
            dma((chunks,)),
            dma((chunks,)),
            dma((chunks,)),
            dma((2, chunks, ranks - 1)),
            dma((2, chunks, ranks - 1)),
            dma((3, chunks)),
        ],
        compiler_params=pltpu.CompilerParams(
            collective_id=0, has_side_effects=True, vmem_limit_bytes=58 * 2**20
        ),
        name="spectra",
    )(*arrays)


def shared_out(block, ways):
    local_count = block.shape[2] // ways
    ring = jnp.concatenate([block[:, :, -halo:], block, block[:, :, :halo]], axis=2)
    width = local_count + 2 * halo
    parts = [ring[:, :, way * local_count : way * local_count + width] for way in range(ways)]
    stacked = jnp.stack(parts)
    stacked = stacked.reshape(ways, block.shape[0], block.shape[1] * width, block.shape[3])
    spare = -stacked.shape[2] % 16
    return jnp.pad(stacked, ((0, 0), (0, 0), (0, spare), (0, 0)))


def chunk_plan(coarse_count, chunks):
    table = theta_table(coarse_count)
    fine_chunk = 2 * coarse_count // chunks
    needed = []
    for chunk in range(chunks):
        used = np.nonzero(table[chunk * fine_chunk : (chunk + 1) * fine_chunk].any(axis=0))[0]
        needed.append((int(used[0]), int(used[-1]) + 1))
    starts = [0] + [end for _, end in needed[:-1]]
    return [(start, end) for start, (_, end) in zip(starts, needed)], needed


def local(child_spectra, child_ids, translators, trans_index):
    ways = lax.axis_size("dir")
    rows = lax.axis_size("box")
    theta_coarse, phi_coarse, width = child_spectra.shape[1:]
    row_children = child_ids.shape[0]
    theta_fine = 2 * theta_coarse
    local_coarse = phi_coarse // ways
    local_fine = 2 * local_coarse
    parents_all = trans_index.shape[0]
    parents = parents_all // rows
    chunks = next(count for count in (3, 2, 1) if theta_fine % (count * rows) == 0)
    fine_chunk = theta_fine // chunks
    theta_local = fine_chunk // rows
    points = theta_local * local_fine
    box_rank = lax.axis_index("box")
    dir_rank = lax.axis_index("dir")
    segments, needed = chunk_plan(theta_coarse, chunks)

    forward = [(source, source + 1) for source in range(rows - 1)]
    ghost_ids = lax.ppermute(child_ids[-straddle:], "box", forward)
    ghost_ids = jnp.where(box_rank > 0, ghost_ids, -8)
    all_ids = jnp.concatenate([ghost_ids, child_ids])
    slots = all_ids // 8 - box_rank * parents
    octants = all_ids % 8
    same = slots[1:] == slots[:-1]
    keeps = jnp.concatenate([jnp.zeros((1,), jnp.float32), same.astype(jnp.float32)])
    upper = octants >= 4
    signs = jnp.where(upper, 1.0, -1.0).astype(jnp.float32)
    mirrored = jnp.where(upper, octants - 4, 3 - octants)
    slot_range = jnp.arange(parents, dtype=jnp.int32)
    lasts = jnp.sum((slots[None, :] <= slot_range[:, None]).astype(jnp.int32), axis=1)

    packed = [shared_out(child_spectra[:, start:end], ways) for start, end in segments]
    first = lax.all_to_all(packed[0], "dir", split_axis=0, concat_axis=0, tiled=True)
    first = first.reshape((row_children,) + first.shape[2:])

    phi_index = (dir_rank * local_fine + jnp.arange(local_fine, dtype=jnp.int32)).astype(
        jnp.float32
    )
    phi_angles = 2.0 * jnp.pi * phi_index / (local_fine * ways)
    cosine, sine = phase_factors(jnp.arange(4, 8, dtype=jnp.int32), theta_fine, phi_angles)

    def lanes(table, chunk):
        part = table[:, chunk * fine_chunk : (chunk + 1) * fine_chunk]
        part = part.reshape(4, fine_chunk * local_fine, 1)
        return jnp.broadcast_to(part, part.shape[:2] + (width // 2,))

    theta_weights = theta_table(theta_coarse).astype(ml_dtypes.bfloat16).astype(np.float64)
    phi_weights = local_phi_table(local_coarse)

    count = translators.shape[1]
    split = translators.reshape(2, count, chunks, rows, theta_local, local_fine)
    own = lax.dynamic_index_in_dim(split, box_rank, 3, keepdims=False)
    own = own.transpose(0, 2, 3, 4, 1).reshape(2 * chunks * points, count)
    chosen = trans_index.reshape(1, -1) - 1 == jnp.arange(count, dtype=jnp.int32)[:, None]
    operators = jnp.dot(own, chosen.astype(jnp.bfloat16), preferred_element_type=jnp.float32)
    operators = operators.astype(jnp.bfloat16)
    operators = operators.reshape(2, chunks, points, parents_all, parents_all)
    operators = operators.transpose(1, 2, 0, 3, 4)
    operators = operators.reshape(chunks, points, 2 * parents_all, parents_all)
    own_shape = (parents, theta_fine, local_fine, width)

    plan, weights = [], []
    for chunk in range(chunks):
        low, high = needed[chunk]
        used = [
            index for index, (start, end) in enumerate(segments) if start < high and end > low
        ]
        tables = []
        for index in used:
            start, end = segments[index]
            table = np.einsum(
                "ht,gj->hgtj",
                theta_weights[chunk * fine_chunk : (chunk + 1) * fine_chunk, start:end],
                phi_weights,
            )
            table = table.reshape(fine_chunk * local_fine, -1)
            table = np.pad(table, ((0, 0), (0, -table.shape[1] % 16)))
            tables.append(jnp.asarray(table.astype(ml_dtypes.bfloat16)))
        plan.append(used)
        weights.append(tables)
    parent_spectra, incoming = spectra(
        first,
        packed[1:],
        (keeps, mirrored, signs, lasts),
        plan,
        weights,
        [lanes(cosine, chunk) for chunk in range(chunks)],
        [lanes(sine, chunk) for chunk in range(chunks)],
        [operators[chunk] for chunk in range(chunks)],
        parents,
        rows,
    )
    incoming = incoming.reshape(rows, chunks, theta_local, local_fine, parents, width)
    incoming = incoming.transpose(4, 1, 0, 2, 3, 5).reshape(own_shape)
    return parent_spectra.reshape(own_shape), incoming


def solution(mesh):
    return jax.shard_map(
        local,
        mesh=mesh,
        in_specs=(P(("box", "dir"), None, None, None), P("box"), P(None, None, None, "dir"), P()),
        out_specs=(P("box", None, "dir", None), P("box", None, "dir", None)),
        check_vma=False,
    )
```

time: 372 us -> 317 us (0.85)
  waiting for transfers between devices: 35.4 us -> 0.01 us
  starting transfers between devices: 23.8 us -> 6.74 us
  Pallas kernels: 244 us -> 227 us
  local copies, waits for them, and re-layouts: 57.1 us -> 63.9 us
  other arithmetic: 8.92 us -> 13.6 us
    all_to_all x3 -> x1, waiting for transfers between devices: 35.4 us -> 0.01 us  [local(): lax.all_to_all(packed[0], 'dir', split_axis=0, concat_axis=0, tiled=True)]
    pallas_call x4 -> x1, Pallas kernels: 244 us -> 227 us  [spectra(): pl.pallas_call(functools.partial(spectra_kernel, chunks, parents, ranks,...]
    all_to_all x3 -> x1, starting transfers between devices: 13.8 us -> 4.7 us  [local(): lax.all_to_all(packed[0], 'dir', split_axis=0, concat_axis=0, tiled=True)]
    ppermute x3 -> x0, starting transfers between devices: 8.02 us -> none  [local(): ghosts.append(lax.ppermute(got[-straddle:], 'box', forward))]
    another operation x0 -> x8, local copies, waits for them, and re-layouts: none -> 4.58 us  [shared_out(): stacked = jnp.stack(parts)]
    slice x9 -> x6, local copies, waits for them, and re-layouts: 4.28 us -> 0.34 us  [local(): child_spectra[:, start:end]]
    unnamed x67 -> x52, local copies, waits for them, and re-layouts: 11.4 us -> 9.26 us
  transfers between devices with their start and end apart: 7 -> 2, of which waited for: 3 -> 0; matrix products, arithmetic and copies ran while one was open for 11% -> 19% of each run, Pallas kernels for 3% -> 0%
where the time goes in v3:
time: 317 us; the launch traced here: 316 us
  Pallas kernels  227 us (72%)
  local copies, waits for them, and re-layouts  63.9 us (20%)
  other arithmetic  13.6 us (4%)
  starting transfers between devices  6.74 us (2%)
  matrix products  3.65 us (1%)
    pallas_call x1, Pallas kernels, spectra(): pl.pallas_call(functools.partial(spectra_kernel, chunks, parents, ranks,...  227 us
    broadcast_in_dim x12, local copies, waits for them, and re-layouts, lanes(): return jnp.broadcast_to(part, part.shape[:2] + (width // 2,))  12.9 us
    reshape x2, local copies, waits for them, and re-layouts, local(): operators = operators.reshape(2, chunks, points, parents_all, parents_all)  11.1 us
    unnamed x52, local copies, waits for them, and re-layouts  9.26 us
  transfers between devices with their start and end apart: 2, of which 0 were waited for; matrix products, arithmetic and copies ran while one was open for 19% of the time, Pallas kernels for 0%

profile of v3, /device:TPU:16, one launch (start us, length us, event | category | flops | bytes accessed | tf_op | source)
XLA Modules:
  0.0 316.2 jit_solution(5828020728142534562)
XLA Ops:
  0.7 1.4 slice.141
  2.0 2.0 collective-permute-start
  4.1 1.3 fusion.36
  5.4 1.2 fusion.37
  8.4 2.1 fusion.6
  10.4 4.7 %all-to-all-start = ((bf16[4,8,208,256]{3,1,2,0:T(8,128)(2,1)}), bf16[4,8,208,256]{3,1,2,0:T(8,128)(2,1)}, u32[]{:S(2)}, u32[]{:S(2)}) async-start(bf16[4,8,208,256]{3,1,2,0:T(8,128)(2,1)} %fusion.6), calls=%async_computation | async-start | bytes 6815744 | tf_op jit(solution)/shard_map/all_to_all | solution.py:389
  16.4 1.7 fusion.32
  19.3 2.7 fusion.33
  23.5 1.5 copy.75
  25.0 1.5 copy.79
  31.5 1.4 fusion.39
  32.9 1.4 broadcast_in_dim.71
  34.3 1.4 broadcast_in_dim.69
  45.4 3.6 %convolution_convert_fusion = bf16[288,4096]{1,0:T(8,128)(2,1)} fusion(bf16[288,316]{1,0:T(8,128)(2,1)S(1)} %bitcast.56, s32[4096]{0:T(1024)} %sub.56), kind=kOutput, calls=%fused_computation.5 | convolution fusion | flops 748011520 | bytes 2557696 | tf_op jit(solution)/shard_map/dot_general | solution.py:411
  49.0 7.6 %reshape.327 = bf16[2,3,48,64,64]{4,3,2,1,0:T(8,128)(2,1)} reshape(bf16[288,4096]{1,0:T(8,128)(2,1)} %convolution_convert_fusion) | data formatting | bytes 4718592 | tf_op jit(solution)/shard_map/reshape | solution.py:413
  56.6 3.5 %copy.81 = bf16[2,3,48,64,64]{4,3,0,2,1:T(8,128)(2,1)S(1)} copy(bf16[2,3,48,64,64]{4,3,2,1,0:T(8,128)(2,1)} %reshape.327) | data formatting | bytes 4718592 | tf_op jit(solution)/shard_map/reshape | solution.py:413
  60.1 1.7 pad_maximum_fusion.refs_1_
  61.8 1.3 fusion.14.refs_2_
  63.2 2.5 fusion.31
  68.9 4.4 %copy.44 = bf16[4,8,208,256]{3,2,1,0:T(8,128)(2,1)} copy(bf16[4,8,208,256]{3,1,2,0:T(8,128)(2,1)} %all-to-all-done) | data formatting | bytes 6815744 | tf_op jit(solution)/shard_map/all_to_all | solution.py:389
  74.5 1.2 broadcast_in_dim.70.refs_13_
  80.3 227.3 %spectra.1 = (bf16[8,1152,256]{2,1,0:T(8,128)(2,1)}, bf16[8,1152,256]{2,1,0:T(8,128)(2,1)}) custom-call(bf16[32,208,256]{2,1,0:T(8,128)(2,1)} %bitcast.35, bf16[4,8,144,256]{3,2,1,0:T(8,128)(2,1)} %pad_maximum_fusion.refs_1_, bf16[4,8,96,256]{3,2,1,0:T(8,128)(2,1)} %fusion.14.refs_2_, f32[35]{0:T(128)} %add_convert_fusion.refs_3_, ...), custom_call_target="tpu_custom_call" | custom-call | tf_op jit(solution)/shard_map/spectra/pallas_call | solution.py:303
  307.7 5.8 %copy.64 = bf16[8,3,8,2,24,256]{5,4,3,2,1,0:T(8,128)(2,1)} copy(bf16[8,3,8,2,24,256]{5,0,4,3,1,2:T(8,128)(2,1)} %bitcast.42) | data formatting | bytes 9437184 | tf_op jit(solution)/shard_map/transpose | solution.py:450
  313.5 2.2 copy.83
  (99 shorter events, 29.6 us)
Async XLA Ops:
  0.6 44.7 %copy-start = (bf16[2,316,48,24]{1,3,2,0:T(8,128)(2,1)S(1)}, bf16[2,316,48,24]{1,3,2,0:T(8,128)(2,1)}, u32[]{:S(2)}) copy-start(bf16[2,316,48,24]{1,3,2,0:T(8,128)(2,1)} %param.11) | copy-start | bytes 4368388
  0.6 4.7 %copy-start.2 = (bf16[8,24,48,256]{3,2,1,0:T(8,128)(2,1)S(1)}, bf16[8,24,48,256]{3,2,1,0:T(8,128)(2,1)}, u32[]{:S(2)}) copy-start(bf16[8,24,48,256]{3,2,1,0:T(8,128)(2,1)} %param.9) | copy-start | bytes 14155780
  2.0 63.7 %collective-permute-start = (s32[3]{0:T(128)}, s32[3]{0:T(128)}, u32[]{:S(2)}, u32[]{:S(2)}) collective-permute-start(s32[3]{0:T(128)} %slice.141), channel_id=1, source_target_pairs={{0,4},{4,8},{8,12},{12,16},{16,20},{20,24},{24,28},{1,5},{5,9},{9,... | collective-permute-start | bytes 44 | tf_op jit(solution)/shard_map/ppermute | solution.py:375
  5.4 1.6 slice-start.2
  10.4 58.5 %all-to-all-start = ((bf16[4,8,208,256]{3,1,2,0:T(8,128)(2,1)}), bf16[4,8,208,256]{3,1,2,0:T(8,128)(2,1)}, u32[]{:S(2)}, u32[]{:S(2)}) async-start(bf16[4,8,208,256]{3,1,2,0:T(8,128)(2,1)} %fusion.6), calls=%async_computation | async-start | bytes 6815744 | tf_op jit(solution)/shard_map/all_to_all | solution.py:389
  19.3 17.3 %slice-start.3 = ((bf16[8,24,48,256]{3,2,1,0:T(8,128)(2,1)}), bf16[8,5,48,256]{3,2,1,0:T(8,128)(2,1)S(1)}, s32[]{:S(2)}) async-start(bf16[8,24,48,256]{3,2,1,0:T(8,128)(2,1)} %param.9), calls=%async_computation.4 | async-start | bytes 1966080 | tf_op jit(solution)/shard_map/slice | solution.py:388
  36.5 3.3 %copy-start.4 = (bf16[8,5,18,256]{3,2,1,0:T(8,128)(2,1)S(1)}, bf16[8,5,18,256]{3,2,1,0:T(8,128)(2,1)}, u32[]{:S(2)}) copy-start(bf16[8,5,18,256]{3,2,1,0:T(8,128)(2,1)} %get-tuple-element.13) | copy-start | bytes 1105924
  37.0 4.5 %slice-start.4 = ((bf16[8,24,48,256]{3,2,1,0:T(8,128)(2,1)}), bf16[8,8,48,256]{3,2,1,0:T(8,128)(2,1)S(1)}, s32[]{:S(2)}) async-start(bf16[8,24,48,256]{3,2,1,0:T(8,128)(2,1)} %param.9), calls=%async_computation.5 | async-start | bytes 3145728 | tf_op jit(solution)/shard_map/slice | solution.py:388
  39.8 3.0 slice-start
  41.5 1.3 slice-start.1
  56.6 3.5 %copy-start.3 = (bf16[1,8,144,256]{3,2,1,0:T(8,128)(2,1)S(1)}, bf16[1,8,144,256]{3,2,1,0:T(8,128)(2,1)}, u32[]{:S(2)}) copy-start(bf16[1,8,144,256]{3,2,1,0:T(8,128)(2,1)} %copy.52) | copy-start | bytes 1769476
  60.1 1.7 copy-start.5
  60.1 1.7 copy-start.6
  60.1 1.7 copy-start.7
  60.1 1.7 copy-start.8
  63.2 3.2 %copy-start.13 = (s32[32]{0:T(128)S(1)}, s32[32]{0:T(128)}, u32[]{:S(2)}) copy-start(s32[32]{0:T(128)} %param.10) | copy-start | bytes 388
  68.9 4.4 %copy-start.12 = (f32[4,384]{1,0:T(4,128)S(1)}, f32[4,384]{1,0:T(4,128)}, u32[]{:S(2)}) copy-start(f32[4,384]{1,0:T(4,128)} %broadcast_in_dim.67) | copy-start | bytes 18436
  68.9 5.6 %copy-start.11 = (f32[4,384]{1,0:T(4,128)S(1)}, f32[4,384]{1,0:T(4,128)}, u32[]{:S(2)}) copy-start(f32[4,384]{1,0:T(4,128)} %broadcast_in_dim.69) | copy-start | bytes 18436
  68.9 6.8 %copy-start.10 = (f32[4,384]{1,0:T(4,128)S(1)}, f32[4,384]{1,0:T(4,128)}, u32[]{:S(2)}) copy-start(f32[4,384]{1,0:T(4,128)} %broadcast_in_dim.71) | copy-start | bytes 18436
  68.9 7.9 %copy-start.9 = (f32[4,384]{1,0:T(4,128)S(1)}, f32[4,384]{1,0:T(4,128)}, u32[]{:S(2)}) copy-start(f32[4,384]{1,0:T(4,128)} %broadcast_in_dim.73) | copy-start | bytes 18436
  307.7 5.8 %slice-start.5 = ((s8[4718592]{0:T(1024)(128)(4,1)}), s8[4194304]{0:T(1024)(128)(4,1)S(1)}, s32[]{:S(2)}) async-start(s8[4718592]{0:T(1024)(128)(4,1)} %bitcast.39), calls=%async_computation.6 | async-start | bytes 8388608
  307.7 5.8 %slice-start.6 = ((s8[4718592]{0:T(1024)(128)(4,1)}), s8[524288]{0:T(1024)(128)(4,1)S(1)}, s32[]{:S(2)}) async-start(s8[4718592]{0:T(1024)(128)(4,1)} %bitcast.39), calls=%async_computation.7 | async-start | bytes 1048576
  313.4 2.7 copy-start.1

commit v4 on v3

--- a/solution.py
+++ b/solution.py
@@ -42,32 +42,16 @@
     return table_rows
 
 
-def phase_factors(octants, theta_count, phi_angles):
-    theta_angles = jnp.pi * (jnp.arange(theta_count, dtype=jnp.float32) + 0.5) / theta_count
-    sign_x = ((octants % 2).astype(jnp.float32) * 2.0 - 1.0)[:, None, None]
-    sign_y = ((octants // 2 % 2).astype(jnp.float32) * 2.0 - 1.0)[:, None, None]
-    sign_z = ((octants // 4).astype(jnp.float32) * 2.0 - 1.0)[:, None, None]
-    sine_theta = jnp.sin(theta_angles)[None, :, None]
-    cosine_theta = jnp.cos(theta_angles)[None, :, None]
-    angle_sum = wave_shift * (
-        sign_x * sine_theta * jnp.cos(phi_angles)[None, None, :]
-        + sign_y * sine_theta * jnp.sin(phi_angles)[None, None, :]
-        + sign_z * cosine_theta
-    )
-    return (jnp.cos(angle_sum), jnp.sin(angle_sum))
-
-
 def spectra_kernel(chunks, parents, ranks, ways, plan, *refs):
-    first, packed, refs = refs[0], refs[1:chunks], refs[chunks:]
+    packed, refs = refs[:chunks], refs[chunks:]
     keeps, octants, signs, lasts, refs = *refs[:4], refs[4:]
     used = sum(len(pieces) for pieces in plan)
     flat_weights, refs = refs[:used], refs[used:]
-    cosine, sine, refs = refs[:chunks], refs[chunks : 2 * chunks], refs[2 * chunks :]
-    operators, refs = refs[:chunks], refs[chunks:]
+    waves, table, choice, refs = *refs[:3], refs[3:]
     own_out, out, refs = refs[0], refs[1], refs[2:]
     columns, refs = refs[:chunks], refs[chunks:]
-    running, staged, sent, held, ready = refs[:5]
-    dir_send, dir_recv, ghost_send, ghost_recv, keep_sem, box_send, box_recv, own_sem = refs[5:]
+    running, staged, sent, held, ready, cosine, sine, operators, picked = refs[:9]
+    dir_send, dir_recv, ghost_send, ghost_recv, keep_sem, box_send, box_recv, own_sem = refs[9:]
     weights = []
     for pieces in plan:
         weights.append(flat_weights[: len(pieces)])
@@ -98,26 +82,20 @@
     def dir_copy(piece, offset):
         target = lax.rem(side + offset, ways)
         return pltpu.make_async_remote_copy(
-            src_ref=packed[piece - 1].at[target],
+            src_ref=packed[piece].at[target],
             dst_ref=columns[piece].at[pl.ds(straddle + side * share, share)],
-            send_sem=dir_send.at[piece - 1, offset - 1],
-            recv_sem=dir_recv.at[piece - 1, offset - 1],
+            send_sem=dir_send.at[piece, offset - 1],
+            recv_sem=dir_recv.at[piece, offset - 1],
             **to_dir(target),
         )
 
     def dir_kept(piece):
-        if piece == 0:
-            source, landing = first, columns[0].at[pl.ds(straddle, children - straddle)]
-        else:
-            source = packed[piece - 1].at[side]
-            landing = columns[piece].at[pl.ds(straddle + side * share, share)]
+        source = packed[piece].at[side]
+        landing = columns[piece].at[pl.ds(straddle + side * share, share)]
         return pltpu.make_async_copy(source, landing, keep_sem.at[piece])
 
     def ghost_copy(piece):
-        if piece == 0:
-            source = first.at[pl.ds(children - 2 * straddle, straddle)]
-        else:
-            source = columns[piece].at[pl.ds(children - straddle, straddle)]
+        source = columns[piece].at[pl.ds(children - straddle, straddle)]
         return pltpu.make_async_remote_copy(
             src_ref=source,
             dst_ref=columns[piece].at[pl.ds(0, straddle)],
@@ -168,9 +146,7 @@
         def _():
             ghost_copy(piece).wait_recv()
 
-    forward_ghosts(0)
-    dir_kept(0).start()
-    for piece in range(1, chunks):
+    for piece in range(chunks):
         for offset in range(1, ways):
             dir_copy(piece, offset).start()
         dir_kept(piece).start()
@@ -181,13 +157,46 @@
             columns[piece][0:straddle] = jnp.zeros((straddle,) + columns[piece].shape[1:], jnp.bfloat16)
 
     running[0] = jnp.zeros(running.shape[1:], jnp.float32)
+    strip = 32
+
+    @pl.loop(0, chunks * points // strip)
+    def _(index):
+        span = pl.ds(pl.multiple_of(index * strip, strip), strip)
+        along_x, along_y, along_z = waves[0, span], waves[1, span], waves[2, span]
+        for octant in range(4):
+            angle = along_z + along_x if octant % 2 else along_z - along_x
+            angle = angle + along_y if octant // 2 else angle - along_y
+            cosine[octant, span] = jnp.cos(angle)
+            sine[octant, span] = jnp.sin(angle)
+
+    everyone = choice.shape[0]
+    entries = lax.broadcasted_iota(jnp.int32, (table.shape[2], everyone), 0)
+
+    @pl.loop(0, everyone // 16)
+    def _(batch):
+        low = pl.multiple_of(batch * 16, 16)
+        rows_of = choice[pl.ds(low, 16)]
+        for member in range(16):
+            chosen = (entries == rows_of[member : member + 1] - 1).astype(jnp.bfloat16)
+            for part in range(2):
+                picked[part, member] = jnp.dot(
+                    table[part], chosen, preferred_element_type=jnp.float32
+                )
+
+        @pl.loop(0, table.shape[1] // 8)
+        def _(tile):
+            start = pl.multiple_of(tile * 8, 8)
+            for part in range(2):
+                block = jnp.swapaxes(picked[part, :, pl.ds(start, 8), :], 0, 1)
+                operators[pl.ds(start, 8), pl.ds(part * everyone + low, 16), :] = block.astype(
+                    jnp.bfloat16
+                )
 
     for chunk in range(chunks):
         dir_kept(chunk).wait()
-        if chunk > 0:
-            for offset in range(1, ways):
-                dir_copy(chunk, offset).wait_recv()
-            forward_ghosts(chunk)
+        for offset in range(1, ways):
+            dir_copy(chunk, offset).wait_recv()
+        forward_ghosts(chunk)
         await_ghosts(chunk)
 
         @pl.loop(0, children)
@@ -200,8 +209,9 @@
                 lifted = part if lifted is None else lifted + part
             octant = octants[child]
             keep = keeps[child]
-            turn_cos = cosine[chunk][octant]
-            turn_sin = sine[chunk][octant] * signs[child]
+            span = pl.ds(chunk * points, points)
+            turn_cos = cosine[octant, span, :]
+            turn_sin = sine[octant, span, :] * signs[child]
             real_part = lifted[:, :half]
             imag_part = lifted[:, half:]
             running[child + 1, :, :half] = (
@@ -232,7 +242,7 @@
         for offset in order:
             box_copy(0, chunk, offset).wait_recv()
         box_kept(0, chunk).wait()
-        table = operators[chunk]
+        first_point = chunk * (rows // parents)
 
         @pl.loop(0, rows // (2 * parents))
         def _(pair):
@@ -244,7 +254,7 @@
                 spectra = jnp.concatenate([value[low : low + parents] for value in both], axis=0)
                 spectra = spectra.astype(jnp.bfloat16)
                 product = jnp.dot(
-                    table[2 * pair + member], spectra, preferred_element_type=jnp.float32
+                    operators[first_point + 2 * pair + member], spectra, preferred_element_type=jnp.float32
                 )
                 count = product.shape[0] // 2
                 direct, cross = product[:count], product[count:]
@@ -278,27 +288,28 @@
         def _():
             ghost_copy(chunk).wait_send()
 
-        if chunk > 0:
-            for offset in range(1, ways):
-                dir_copy(chunk, offset).wait_send()
+        for offset in range(1, ways):
+            dir_copy(chunk, offset).wait_send()
         for phase in range(2):
             for offset in order:
                 box_copy(phase, chunk, offset).wait_send()
 
 
-def spectra(first, packed, scalars, plan, weights, cosine, sine, operators, parents, ranks):
+def spectra(packed, scalars, plan, weights, waves, table, choice, parents, ranks):
     chunks = len(plan)
     ways = packed[0].shape[0]
-    children = first.shape[0] + straddle
-    width = first.shape[-1]
+    children = ways * packed[0].shape[1] + straddle
+    width = packed[0].shape[-1]
     points = weights[0][0].shape[0]
     rows = points * parents // ranks
     whole = (ranks, chunks * rows, width)
-    arrays = [first, *packed, *scalars, *sum(weights, []), *cosine, *sine, *operators]
+    arrays = [*packed, *scalars, *sum(weights, []), waves, table, choice]
     in_specs = [pl.BlockSpec(memory_space=pl.ANY)] * chunks
     in_specs += [pl.BlockSpec(memory_space=pltpu.SMEM)] * len(scalars)
     in_specs += [pl.BlockSpec(memory_space=pltpu.VMEM)] * (len(arrays) - len(in_specs))
-    piece_rows = [first.shape[1]] + [piece.shape[2] for piece in packed]
+    piece_rows = [piece.shape[2] for piece in packed]
+    everyone = choice.shape[0]
+    turns = pltpu.VMEM((4,) + waves.shape[1:], jnp.float32)
     dma = pltpu.SemaphoreType.DMA
     return pl.pallas_call(
         functools.partial(spectra_kernel, chunks, parents, ranks, ways, plan),
@@ -315,8 +326,12 @@
             pltpu.VMEM((chunks, ranks * rows, width), jnp.bfloat16),
             pltpu.VMEM(whole, jnp.bfloat16),
             pltpu.VMEM(whole, jnp.bfloat16),
-            dma((chunks - 1, ways - 1)),
-            dma((chunks - 1, ways - 1)),
+            turns,
+            turns,
+            pltpu.VMEM((table.shape[1], 2 * everyone, everyone), jnp.bfloat16),
+            pltpu.VMEM((2, 16, table.shape[1], everyone), jnp.float32),
+            dma((chunks, ways - 1)),
+            dma((chunks, ways - 1)),
             dma((chunks,)),
             dma((chunks,)),
             dma((chunks,)),
@@ -386,19 +401,20 @@
     lasts = jnp.sum((slots[None, :] <= slot_range[:, None]).astype(jnp.int32), axis=1)
 
     packed = [shared_out(child_spectra[:, start:end], ways) for start, end in segments]
-    first = lax.all_to_all(packed[0], "dir", split_axis=0, concat_axis=0, tiled=True)
-    first = first.reshape((row_children,) + first.shape[2:])
-
-    phi_index = (dir_rank * local_fine + jnp.arange(local_fine, dtype=jnp.int32)).astype(
-        jnp.float32
-    )
-    phi_angles = 2.0 * jnp.pi * phi_index / (local_fine * ways)
-    cosine, sine = phase_factors(jnp.arange(4, 8, dtype=jnp.int32), theta_fine, phi_angles)
-
-    def lanes(table, chunk):
-        part = table[:, chunk * fine_chunk : (chunk + 1) * fine_chunk]
-        part = part.reshape(4, fine_chunk * local_fine, 1)
-        return jnp.broadcast_to(part, part.shape[:2] + (width // 2,))
+
+    place = (theta_fine, local_fine, width // 2)
+    theta_index = lax.broadcasted_iota(jnp.int32, place, 0).astype(jnp.float32)
+    phi_index = lax.broadcasted_iota(jnp.int32, place, 1) + dir_rank * local_fine
+    theta_angles = jnp.pi * (theta_index + 0.5) / theta_fine
+    phi_angles = 2.0 * jnp.pi * phi_index.astype(jnp.float32) / (local_fine * ways)
+    sine_theta = wave_shift * jnp.sin(theta_angles)
+    waves = jnp.stack(
+        [
+            sine_theta * jnp.cos(phi_angles),
+            sine_theta * jnp.sin(phi_angles),
+            wave_shift * jnp.cos(theta_angles),
+        ]
+    ).reshape(3, theta_fine * local_fine, width // 2)
 
     theta_weights = theta_table(theta_coarse).astype(ml_dtypes.bfloat16).astype(np.float64)
     phi_weights = local_phi_table(local_coarse)
@@ -406,13 +422,8 @@
     count = translators.shape[1]
     split = translators.reshape(2, count, chunks, rows, theta_local, local_fine)
     own = lax.dynamic_index_in_dim(split, box_rank, 3, keepdims=False)
-    own = own.transpose(0, 2, 3, 4, 1).reshape(2 * chunks * points, count)
-    chosen = trans_index.reshape(1, -1) - 1 == jnp.arange(count, dtype=jnp.int32)[:, None]
-    operators = jnp.dot(own, chosen.astype(jnp.bfloat16), preferred_element_type=jnp.float32)
-    operators = operators.astype(jnp.bfloat16)
-    operators = operators.reshape(2, chunks, points, parents_all, parents_all)
-    operators = operators.transpose(1, 2, 0, 3, 4)
-    operators = operators.reshape(chunks, points, 2 * parents_all, parents_all)
+    own = own.reshape(2, count, chunks * points).transpose(0, 2, 1)
+    table = jnp.pad(own, ((0, 0), (0, -own.shape[1] % 8), (0, -count % 64)))
     own_shape = (parents, theta_fine, local_fine, width)
 
     plan, weights = [], []
@@ -424,25 +435,24 @@
         tables = []
         for index in used:
             start, end = segments[index]
-            table = np.einsum(
+            product = np.einsum(
                 "ht,gj->hgtj",
                 theta_weights[chunk * fine_chunk : (chunk + 1) * fine_chunk, start:end],
                 phi_weights,
             )
-            table = table.reshape(fine_chunk * local_fine, -1)
-            table = np.pad(table, ((0, 0), (0, -table.shape[1] % 16)))
-            tables.append(jnp.asarray(table.astype(ml_dtypes.bfloat16)))
+            product = product.reshape(fine_chunk * local_fine, -1)
+            product = np.pad(product, ((0, 0), (0, -product.shape[1] % 16)))
+            tables.append(jnp.asarray(product.astype(ml_dtypes.bfloat16)))
         plan.append(used)
         weights.append(tables)
     parent_spectra, incoming = spectra(
-        first,
-        packed[1:],
+        packed,
         (keeps, mirrored, signs, lasts),
         plan,
         weights,
-        [lanes(cosine, chunk) for chunk in range(chunks)],
-        [lanes(sine, chunk) for chunk in range(chunks)],
-        [operators[chunk] for chunk in range(chunks)],
+        waves,
+        table,
+        trans_index,
         parents,
         rows,
     )

time: 317 us -> 325 us (1.025)
  Pallas kernels: 227 us -> 263 us
  local copies, waits for them, and re-layouts: 63.9 us -> 46.4 us
  starting transfers between devices: 6.74 us -> 1.91 us
  matrix products: 3.65 us -> 0 us
    pallas_call x1, Pallas kernels: 227 us -> 263 us  [spectra(): pl.pallas_call(functools.partial(spectra_kernel, chunks, parents, ranks,...]
    broadcast_in_dim x12 -> x0, local copies, waits for them, and re-layouts: 12.9 us -> none  [lanes(): return jnp.broadcast_to(part, part.shape[:2] + (width // 2,))]
    reshape x2 -> x0, local copies, waits for them, and re-layouts: 11.1 us -> none  [local(): operators = operators.reshape(2, chunks, points, parents_all, parents_all)]
    another operation x8 -> x12, local copies, waits for them, and re-layouts: 4.58 us -> 9.49 us  [shared_out(): stacked = jnp.stack(parts)]
    all_to_all x1 -> x0, starting transfers between devices: 4.7 us -> none  [local(): lax.all_to_all(packed[0], 'dir', split_axis=0, concat_axis=0, tiled=True)]
    slice x3 -> x0, local copies, waits for them, and re-layouts: 4.57 us -> none  [the longest x1 2.54 us: local(): operators[chunk]]
    all_to_all x1 -> x0, local copies, waits for them, and re-layouts: 4.43 us -> none  [local(): lax.all_to_all(packed[0], 'dir', split_axis=0, concat_axis=0, tiled=True)]
    dot_general x1 -> x0, matrix products: 3.65 us -> none  [local(): jnp.dot(own, chosen.astype(jnp.bfloat16), preferred_element_type=jnp.floa...]
  transfers between devices with their start and end apart: 2 -> 1, of which waited for: 0 -> 0; matrix products, arithmetic and copies ran while one was open for 19% -> 14% of each run, Pallas kernels for 0% -> 0%
where the time goes in v4:
time: 325 us; the launch traced here: 324 us
  Pallas kernels  263 us (81%)
  local copies, waits for them, and re-layouts  46.4 us (14%)
  other arithmetic  11.8 us (4%)
    pallas_call x1, Pallas kernels, spectra(): pl.pallas_call(functools.partial(spectra_kernel, chunks, parents, ranks,...  263 us
    unnamed x58, local copies, waits for them, and re-layouts  12 us
    another operation x12, local copies, waits for them, and re-layouts, shared_out(): stacked = jnp.stack(parts)  9.49 us
    slice x3, local copies, waits for them, and re-layouts, shared_out(): ring[:, :, way * local_count:way * local_count + width]  7.06 us
  transfers between devices with their start and end apart: 1, of which 0 were waited for; matrix products, arithmetic and copies ran while one was open for 14% of the time, Pallas kernels for 0%

profile of v4, /device:TPU:16, one launch (start us, length us, event | category | flops | bytes accessed | tf_op | source)
XLA Modules:
  0.0 324.4 jit_solution(10695935461676382797)
XLA Ops:
  0.6 1.4 slice.111
  2.0 1.9 collective-permute-start
  4.1 1.7 fusion.16
  5.8 1.9 fusion.18
  7.7 2.0 fusion.20
  9.7 2.9 fusion.17
  12.6 1.7 fusion.19
  14.3 2.4 fusion.21
  18.8 1.3 broadcast_multiply_fusion.1
  21.0 1.4 reshape.145
  24.2 1.0 copy.76
  25.2 1.0 copy.80
  34.0 0.9 copy.59
  35.2 1.0 copy.57
  36.5 0.9 copy.58
  39.8 1.1 copy.48
  41.0 1.0 copy.49
  43.5 1.3 pad_maximum_fusion.1.refs_12_
  44.9 1.4 fusion.13.refs_2_
  46.3 1.7 pad_maximum_fusion.refs_1_
  48.1 1.9 fusion.6.refs_0_
  53.1 263.3 %spectra.1 = (bf16[8,1152,256]{2,1,0:T(8,128)(2,1)}, bf16[8,1152,256]{2,1,0:T(8,128)(2,1)}) custom-call(bf16[4,8,208,256]{3,2,1,0:T(8,128)(2,1)} %fusion.6.refs_0_, bf16[4,8,144,256]{3,2,1,0:T(8,128)(2,1)} %pad_maximum_fusion.refs_1_, bf16[4,8,96,256]{3,2,1,0:T(8,128)(2,1)} %fusion.13.refs_2_, f32[35]{0:T(128)} %add_convert_fusion.refs_3_, ...), custom_call_target="tpu_custom_call" | custom-call | tf_op jit(solution)/shard_map/spectra/pallas_call | solution.py:314
  316.4 5.8 %copy.70 = bf16[8,3,8,2,24,256]{5,4,3,2,1,0:T(8,128)(2,1)} copy(bf16[8,3,8,2,24,256]{5,0,4,3,1,2:T(8,128)(2,1)} %bitcast.27) | data formatting | bytes 9437184 | tf_op jit(solution)/shard_map/transpose | solution.py:460
  322.2 2.2 copy.88
  (90 shorter events, 20.1 us)
Async XLA Ops:
  0.6 41.4 %copy-start = (bf16[2,316,48,24]{1,3,2,0:T(8,128)(2,1)S(1)}, bf16[2,316,48,24]{1,3,2,0:T(8,128)(2,1)}, u32[]{:S(2)}) copy-start(bf16[2,316,48,24]{1,3,2,0:T(8,128)(2,1)} %param.11) | copy-start | bytes 4368388
  2.0 47.9 %collective-permute-start = (s32[3]{0:T(128)}, s32[3]{0:T(128)}, u32[]{:S(2)}, u32[]{:S(2)}) collective-permute-start(s32[3]{0:T(128)} %slice.111), channel_id=1, source_target_pairs={{0,4},{4,8},{8,12},{12,16},{16,20},{20,24},{24,28},{1,5},{5,9},{9,... | collective-permute-start | bytes 44 | tf_op jit(solution)/shard_map/ppermute | solution.py:390
  9.7 3.0 copy-start.1
  14.3 13.8 %slice-start = ((bf16[8,24,48,256]{3,2,1,0:T(8,128)(2,1)}), bf16[8,5,48,256]{3,2,1,0:T(8,128)(2,1)S(1)}, s32[]{:S(2)}) async-start(bf16[8,24,48,256]{3,2,1,0:T(8,128)(2,1)} %param.9), calls=%async_computation | async-start | bytes 1966080 | tf_op jit(solution)/shard_map/slice | solution.py:403
  25.2 5.0 %copy-start.12 = (bf16[8,5,18,256]{3,2,1,0:T(8,128)(2,1)S(1)}, bf16[8,5,18,256]{3,2,1,0:T(8,128)(2,1)}, u32[]{:S(2)}) copy-start(bf16[8,5,18,256]{3,2,1,0:T(8,128)(2,1)} %get-tuple-element.10) | copy-start | bytes 1105924
  28.1 3.0 copy-start.11
  28.5 3.5 %slice-start.1 = ((bf16[8,24,48,256]{3,2,1,0:T(8,128)(2,1)}), bf16[8,8,48,256]{3,2,1,0:T(8,128)(2,1)S(1)}, s32[]{:S(2)}) async-start(bf16[8,24,48,256]{3,2,1,0:T(8,128)(2,1)} %param.9), calls=%async_computation.1 | async-start | bytes 3145728 | tf_op jit(solution)/shard_map/slice | solution.py:403
  32.9 2.0 copy-start.6
  34.0 3.5 %slice-start.2 = ((bf16[8,24,48,256]{3,2,1,0:T(8,128)(2,1)}), bf16[8,11,48,256]{3,2,1,0:T(8,128)(2,1)S(1)}, s32[]{:S(2)}) async-start(bf16[8,24,48,256]{3,2,1,0:T(8,128)(2,1)} %param.9), calls=%async_computation.2 | async-start | bytes 4325376 | tf_op jit(solution)/shard_map/slice | solution.py:403
  38.5 2.3 copy-start.2
  39.8 3.1 copy-start.17
  42.1 2.8 copy-start.13
  42.1 2.8 copy-start.14
  42.1 2.8 copy-start.15
  42.1 2.8 copy-start.16
  43.5 2.8 copy-start.7
  43.5 2.8 copy-start.8
  43.5 2.8 copy-start.9
  43.5 2.7 copy-start.10
  46.3 1.7 copy-start.4
  46.3 1.8 copy-start.5
  48.1 2.5 copy-start.18
  316.4 5.8 %slice-start.3 = ((s8[4718592]{0:T(1024)(128)(4,1)}), s8[4194304]{0:T(1024)(128)(4,1)S(1)}, s32[]{:S(2)}) async-start(s8[4718592]{0:T(1024)(128)(4,1)} %bitcast.24), calls=%async_computation.3 | async-start | bytes 8388608
  316.4 5.8 %slice-start.4 = ((s8[4718592]{0:T(1024)(128)(4,1)}), s8[524288]{0:T(1024)(128)(4,1)S(1)}, s32[]{:S(2)}) async-start(s8[4718592]{0:T(1024)(128)(4,1)} %bitcast.24), calls=%async_computation.4 | async-start | bytes 1048576
  (1 other events, 1.2 us)

commit v5 on v4

--- a/solution.py
+++ b/solution.py
@@ -42,8 +42,8 @@
     return table_rows
 
 
-def spectra_kernel(chunks, parents, ranks, ways, plan, *refs):
-    packed, refs = refs[:chunks], refs[chunks:]
+def spectra_kernel(chunks, parents, ranks, ways, plan, bounds, *refs):
+    packed, refs = refs[0], refs[1:]
     keeps, octants, signs, lasts, refs = *refs[:4], refs[4:]
     used = sum(len(pieces) for pieces in plan)
     flat_weights, refs = refs[:used], refs[used:]
@@ -82,7 +82,7 @@
     def dir_copy(piece, offset):
         target = lax.rem(side + offset, ways)
         return pltpu.make_async_remote_copy(
-            src_ref=packed[piece].at[target],
+            src_ref=packed.at[target, :, pl.ds(bounds[piece], bounds[piece + 1] - bounds[piece])],
             dst_ref=columns[piece].at[pl.ds(straddle + side * share, share)],
             send_sem=dir_send.at[piece, offset - 1],
             recv_sem=dir_recv.at[piece, offset - 1],
@@ -90,7 +90,7 @@
         )
 
     def dir_kept(piece):
-        source = packed[piece].at[side]
+        source = packed.at[side, :, pl.ds(bounds[piece], bounds[piece + 1] - bounds[piece])]
         landing = columns[piece].at[pl.ds(straddle + side * share, share)]
         return pltpu.make_async_copy(source, landing, keep_sem.at[piece])
 
@@ -295,24 +295,24 @@
                 box_copy(phase, chunk, offset).wait_send()
 
 
-def spectra(packed, scalars, plan, weights, waves, table, choice, parents, ranks):
+def spectra(packed, scalars, plan, bounds, weights, waves, table, choice, parents, ranks):
     chunks = len(plan)
-    ways = packed[0].shape[0]
-    children = ways * packed[0].shape[1] + straddle
-    width = packed[0].shape[-1]
+    ways = packed.shape[0]
+    children = ways * packed.shape[1] + straddle
+    width = packed.shape[-1]
     points = weights[0][0].shape[0]
     rows = points * parents // ranks
     whole = (ranks, chunks * rows, width)
-    arrays = [*packed, *scalars, *sum(weights, []), waves, table, choice]
-    in_specs = [pl.BlockSpec(memory_space=pl.ANY)] * chunks
+    arrays = [packed, *scalars, *sum(weights, []), waves, table, choice]
+    in_specs = [pl.BlockSpec(memory_space=pl.ANY)]
     in_specs += [pl.BlockSpec(memory_space=pltpu.SMEM)] * len(scalars)
     in_specs += [pl.BlockSpec(memory_space=pltpu.VMEM)] * (len(arrays) - len(in_specs))
-    piece_rows = [piece.shape[2] for piece in packed]
+    piece_rows = [high - low for low, high in zip(bounds, bounds[1:])]
     everyone = choice.shape[0]
     turns = pltpu.VMEM((4,) + waves.shape[1:], jnp.float32)
     dma = pltpu.SemaphoreType.DMA
     return pl.pallas_call(
-        functools.partial(spectra_kernel, chunks, parents, ranks, ways, plan),
+        functools.partial(spectra_kernel, chunks, parents, ranks, ways, plan, bounds),
         in_specs=in_specs,
         out_specs=[pl.BlockSpec(memory_space=pl.ANY)] * 2,
         out_shape=[
@@ -364,8 +364,7 @@
     for chunk in range(chunks):
         used = np.nonzero(table[chunk * fine_chunk : (chunk + 1) * fine_chunk].any(axis=0))[0]
         needed.append((int(used[0]), int(used[-1]) + 1))
-    starts = [0] + [end for _, end in needed[:-1]]
-    return [(start, end) for start, (_, end) in zip(starts, needed)], needed
+    return needed
 
 
 def local(child_spectra, child_ids, translators, trans_index):
@@ -384,7 +383,7 @@
     points = theta_local * local_fine
     box_rank = lax.axis_index("box")
     dir_rank = lax.axis_index("dir")
-    segments, needed = chunk_plan(theta_coarse, chunks)
+    needed = chunk_plan(theta_coarse, chunks)
 
     forward = [(source, source + 1) for source in range(rows - 1)]
     ghost_ids = lax.ppermute(child_ids[-straddle:], "box", forward)
@@ -400,7 +399,9 @@
     slot_range = jnp.arange(parents, dtype=jnp.int32)
     lasts = jnp.sum((slots[None, :] <= slot_range[:, None]).astype(jnp.int32), axis=1)
 
-    packed = [shared_out(child_spectra[:, start:end], ways) for start, end in segments]
+    packed = shared_out(child_spectra, ways)
+    taps = local_coarse + 2 * halo
+    bounds = [0] + [-(-end * taps // 16) * 16 for _, end in needed[:-1]] + [packed.shape[2]]
 
     place = (theta_fine, local_fine, width // 2)
     theta_index = lax.broadcasted_iota(jnp.int32, place, 0).astype(jnp.float32)
@@ -429,26 +430,27 @@
     plan, weights = [], []
     for chunk in range(chunks):
         low, high = needed[chunk]
+        product = np.einsum(
+            "ht,gj->hgtj",
+            theta_weights[chunk * fine_chunk : (chunk + 1) * fine_chunk],
+            phi_weights,
+        )
+        product = product.reshape(fine_chunk * local_fine, -1)
+        product = np.pad(product, ((0, 0), (0, bounds[-1] - product.shape[1])))
+        product = product.astype(ml_dtypes.bfloat16)
         used = [
-            index for index, (start, end) in enumerate(segments) if start < high and end > low
+            index
+            for index in range(chunks)
+            if bounds[index] < high * taps and bounds[index + 1] > low * taps
         ]
-        tables = []
-        for index in used:
-            start, end = segments[index]
-            product = np.einsum(
-                "ht,gj->hgtj",
-                theta_weights[chunk * fine_chunk : (chunk + 1) * fine_chunk, start:end],
-                phi_weights,
-            )
-            product = product.reshape(fine_chunk * local_fine, -1)
-            product = np.pad(product, ((0, 0), (0, -product.shape[1] % 16)))
-            tables.append(jnp.asarray(product.astype(ml_dtypes.bfloat16)))
+        tables = [jnp.asarray(product[:, bounds[index] : bounds[index + 1]]) for index in used]
         plan.append(used)
         weights.append(tables)
     parent_spectra, incoming = spectra(
         packed,
         (keeps, mirrored, signs, lasts),
         plan,
+        bounds,
         weights,
         waves,
         table,

time: 325 us -> 299 us (0.920)
  local copies, waits for them, and re-layouts: 46.4 us -> 23.9 us
    slice x9 -> x0, local copies, waits for them, and re-layouts: 7.08 us -> none  [the longest x3 7.06 us: shared_out(): ring[:, :, way * local_count:way * local_count + width]]
    slice x3 -> x1, local copies, waits for them, and re-layouts: 5.62 us -> 0.04 us  [shared_out(): block[:, :, -halo:]]
    another operation x12 -> x4, local copies, waits for them, and re-layouts: 9.49 us -> 5.04 us  [shared_out(): stacked = jnp.stack(parts)]
    unnamed x58 -> x14, local copies, waits for them, and re-layouts: 12 us -> 8.51 us
  transfers between devices with their start and end apart: 1 -> 1, of which waited for: 0 -> 0; matrix products, arithmetic and copies ran while one was open for 14% -> 6% of each run, Pallas kernels for 0% -> 0%
where the time goes in v5:
time: 299 us; the launch traced here: 298 us
  Pallas kernels  263 us (88%)
  local copies, waits for them, and re-layouts  23.9 us (8%)
  other arithmetic  8.74 us (3%)
    pallas_call x1, Pallas kernels, spectra(): pl.pallas_call(functools.partial(spectra_kernel, chunks, parents, ranks,...  263 us
    unnamed x14, local copies, waits for them, and re-layouts  8.51 us
  transfers between devices with their start and end apart: 1, of which 0 were waited for; matrix products, arithmetic and copies ran while one was open for 6% of the time, Pallas kernels for 0%

profile of v5, /device:TPU:16, one launch (start us, length us, event | category | flops | bytes accessed | tf_op | source)
XLA Modules:
  0.0 298.4 jit_solution(5879697732022424530)
XLA Ops:
  0.6 1.4 slice.35
  2.1 1.9 collective-permute-start
  4.5 0.7 reshape.127
  5.1 5.0 %copy.25 = bf16[8,24,48,256]{3,0,2,1:T(8,128)(2,1)S(1)} copy(bf16[8,24,48,256]{3,2,1,0:T(8,128)(2,1)} %param.9) | data formatting | bytes 9437184 | tf_op args[0]
  10.2 0.5 pad_maximum_fusion.2
  10.7 0.4 copy.31
  11.1 1.6 copy.33
  12.7 1.6 copy.32
  14.2 1.6 copy.34
  15.8 0.7 pad.4.refs_11_
  16.5 1.0 iota.38
  17.8 0.2 iota.40
  18.0 1.3 pad_maximum_fusion.3.refs_10_
  19.4 0.8 copy-done.1
  20.1 0.5 copy-done.2
  20.7 3.5 %pad_maximum_fusion.refs_0_ = bf16[4,8,432,256]{3,2,1,0:T(8,128)(2,1)} fusion(bf16[1,8,432,256]{3,2,1,0:T(8,128)(2,1)S(1)} %copy-done.3, bf16[1,8,432,256]{3,2,1,0:T(8,128)(2,1)S(1)} %copy-done.1, bf16[1,8,432,256]{3,2,1,0:T(8,128)(2,1)S(1)} %copy-done.2, bf16[1,8,432,256]{3,2,1,0:T(8,128)(2,1)S(1)} %copy.31), kind=kLoop, calls=%fused_computation | loop fusion | flops 10616832 | bytes 14155776 | tf_op jit(solution)/shard_map/stack | solution.py:354
  24.2 0.7 broadcast_select_fusion
  24.9 0.6 compare_select_fusion.3
  25.5 0.5 compare_select_fusion.4
  26.0 0.6 convert_reduce_fusion.refs_4_
  26.7 0.7 add_convert_fusion.refs_1_
  27.3 263.1 %spectra.1 = (bf16[8,1152,256]{2,1,0:T(8,128)(2,1)}, bf16[8,1152,256]{2,1,0:T(8,128)(2,1)}) custom-call(bf16[4,8,432,256]{3,2,1,0:T(8,128)(2,1)} %pad_maximum_fusion.refs_0_, f32[35]{0:T(128)} %add_convert_fusion.refs_1_, s32[35]{0:T(128)} %get-tuple-element.16.refs_2_, f32[35]{0:T(128)} %get-tuple-element.6.refs_3_, s32[8]{0:T(128)} %convert_reduce_fusion.refs_4_, ...), custom_call_target="tpu_custom_call" | custom-call | tf_op jit(solution)/shard_map/spectra/pallas_call | solution.py:314
  290.4 5.8 %copy.36 = bf16[8,3,8,2,24,256]{5,4,3,2,1,0:T(8,128)(2,1)} copy(bf16[8,3,8,2,24,256]{5,0,4,3,1,2:T(8,128)(2,1)} %bitcast.21) | data formatting | bytes 9437184 | tf_op jit(solution)/shard_map/transpose | solution.py:462
  296.2 2.2 copy.39
  (22 shorter events, 0.8 us)
Async XLA Ops:
  0.6 15.2 %copy-start = (bf16[2,316,48,24]{1,3,2,0:T(8,128)(2,1)S(1)}, bf16[2,316,48,24]{1,3,2,0:T(8,128)(2,1)}, u32[]{:S(2)}) copy-start(bf16[2,316,48,24]{1,3,2,0:T(8,128)(2,1)} %param.11) | copy-start | bytes 4368388
  2.1 22.1 %collective-permute-start = (s32[3]{0:T(128)}, s32[3]{0:T(128)}, u32[]{:S(2)}, u32[]{:S(2)}) collective-permute-start(s32[3]{0:T(128)} %slice.35), channel_id=1, source_target_pairs={{0,4},{4,8},{8,12},{12,16},{16,20},{20,24},{24,28},{1,5},{5,9},{9,... | collective-permute-start | bytes 44 | tf_op jit(solution)/shard_map/ppermute | solution.py:389
  16.5 2.8 copy-start.3
  18.0 2.1 copy-start.1
  18.0 2.6 copy-start.2
  20.7 4.2 %copy-start.5 = (s32[32]{0:T(128)S(1)}, s32[32]{0:T(128)}, u32[]{:S(2)}) copy-start(s32[32]{0:T(128)} %param.10) | copy-start | bytes 388
  290.4 5.8 %copy-start.4 = (bf16[8,1152,256]{2,1,0:T(8,128)(2,1)S(1)}, bf16[8,1152,256]{2,1,0:T(8,128)(2,1)}, u32[]{:S(2)}) copy-start(bf16[8,1152,256]{2,1,0:T(8,128)(2,1)} %get-tuple-element.4) | copy-start | bytes 14155780
